TPU v7x, 512 devices: a whole 4x8x8 slice. The times are simulated.
512 devices in a mesh: dp: 64 (over x, z, core), head: 8 (over y).
Axes of the slice: x: 4, y: 8, z: 8, core: 2. Of those that a mesh axis runs over, the one named last changes fastest.
Arguments:
- projected: bfloat16 [8192, 7168], P(('dp', 'head')), may hold values from -64 to 64
- grad_output: bfloat16 [8192, 5120], P(('dp', 'head')), may hold values from -4 to 4
- prompt_cache: bfloat16 [32768, 2048], P('dp', 'head'), may hold values from -6 to 6
- segment_ids: int32 [64, 128], P('dp'), may hold values from 0 to 3, never falling along the last dimension, each value on 1 to 64 neighbouring positions
- segment_prompt: int32 [64, 4], P('dp'), may hold values from 0 to 63, as said below
Outputs:
- attention_out: bfloat16 [8192, 5120], P(('dp', 'head'))
- grad_projected: bfloat16 [8192, 7168], P(('dp', 'head'))
- grad_prompt_cache: bfloat16 [32768, 2048], P('dp', 'head')
Inputs may be any that keep to these rules, and one draw needn't show every extreme that they name: `segment_ids`: on each index of dp the response numbers never fall, all 4 responses appear, each with 1 to 64 tokens. `segment_prompt`: the prompt of a response on dp index d is (d + o) mod 64 with o between -4 and 4; both ends occur.
All inputs are finite; a program needn't handle non-finite values.
Results may differ from a plain program's by a relative error of at most 0.04.
Values may be sent and summed in bfloat16 or wider, within the bound.
A program may use at most 64 MiB of HBM per device.

v0:
```python
import jax
import jax.numpy as jnp
from jax import lax
from jax.sharding import PartitionSpec as P

HEADS = 40
KV_HEADS = 8
HEAD_DIM = 128
PROMPT_LEN = 512
SEGS = 4
REACH = 4
SEG_MOST = 64


def passed_along(block, axis, distance):
    devices = range(lax.axis_size(axis))
    route = [((i - distance) % len(devices), i) for i in devices]
    return lax.ppermute(block, axis, route)


def product(form, left, right):
    return jnp.einsum(form, left, right, preferred_element_type=jnp.float32)


def place(window, start, full_len, axis, fill):
    shape = list(window.shape)
    shape[axis] = full_len
    base = jnp.full(tuple(shape), fill, window.dtype)
    return lax.dynamic_update_slice_in_dim(base, window, start, axis)


def attend(queries, keys_now, values_now, dout, segment_row, prompt_blocks):
    row_count = queries.shape[0]
    width = SEG_MOST
    score_scale = queries.shape[-1] ** (-0.5)
    position = lax.iota(jnp.int32, row_count)
    self_mask = (segment_row[:, None] == segment_row[None, :]) & (
        position[None, :] <= position[:, None]
    )
    self_scores = jnp.where(
        self_mask, product("tkgh,ukh->kgtu", queries, keys_now) * score_scale, -jnp.inf
    )
    prompt_keys = prompt_blocks[:, :, :, 0]
    prompt_values = prompt_blocks[:, :, :, 1]
    starts = []
    windows = []
    row_max = jnp.max(self_scores, axis=-1)
    for segment in range(SEGS):
        first = jnp.sum((segment_row < segment).astype(jnp.int32))
        start = jnp.clip(first, 0, row_count - width)
        live = lax.dynamic_slice_in_dim(segment_row, start, width, 0) == segment
        query_win = lax.dynamic_slice_in_dim(queries, start, width, 0)
        scores = jnp.where(
            live[None, None, :, None],
            product("tkgh,lkh->kgtl", query_win, prompt_keys[segment]) * score_scale,
            -jnp.inf,
        )
        row_max = jnp.maximum(
            row_max, place(jnp.max(scores, axis=-1), start, row_count, 2, -jnp.inf)
        )
        starts.append(start)
        windows.append(scores)
    self_exp = jnp.exp(self_scores - row_max[..., None])
    row_total = jnp.sum(self_exp, axis=-1)
    exps = []
    for segment in range(SEGS):
        start = starts[segment]
        max_win = lax.dynamic_slice_in_dim(row_max, start, width, 2)
        expo = jnp.exp(windows[segment] - max_win[..., None])
        row_total = row_total + place(jnp.sum(expo, axis=-1), start, row_count, 2, 0.0)
        exps.append(expo)
    self_weight = self_exp / row_total[..., None]
    self_rounded = self_weight.astype(jnp.bfloat16)
    attended = product("kgtu,ukh->tkgh", self_rounded, values_now)
    weights = []
    for segment in range(SEGS):
        start = starts[segment]
        total_win = lax.dynamic_slice_in_dim(row_total, start, width, 2)
        weight = exps[segment] / total_win[..., None]
        rounded = weight.astype(jnp.bfloat16)
        attended = attended + place(
            product("kgtl,lkh->tkgh", rounded, prompt_values[segment]), start, row_count, 0, 0.0
        )
        weights.append((weight, rounded))
    attended = attended.astype(jnp.bfloat16)
    dot_term = jnp.sum(dout.astype(jnp.float32) * attended.astype(jnp.float32), axis=-1)
    delta = jnp.transpose(dot_term, (1, 2, 0))
    self_grad = (
        self_weight * (product("tkgh,ukh->kgtu", dout, values_now) - delta[..., None]) * score_scale
    ).astype(jnp.bfloat16)
    query_grad = product("kgtu,ukh->tkgh", self_grad, keys_now)
    prompt_terms = []
    for segment in range(SEGS):
        start = starts[segment]
        weight, rounded = weights[segment]
        dout_win = lax.dynamic_slice_in_dim(dout, start, width, 0)
        query_win = lax.dynamic_slice_in_dim(queries, start, width, 0)
        delta_win = lax.dynamic_slice_in_dim(delta, start, width, 2)
        prefix_grad = (
            weight
            * (product("tkgh,lkh->kgtl", dout_win, prompt_values[segment]) - delta_win[..., None])
            * score_scale
        ).astype(jnp.bfloat16)
        query_grad = query_grad + place(
            product("kgtl,lkh->tkgh", prefix_grad, prompt_keys[segment]), start, row_count, 0, 0.0
        )
        prompt_dkey = product("kgtl,tkgh->lkh", prefix_grad, query_win)
        prompt_dvalue = product("kgtl,tkgh->lkh", rounded, dout_win)
        prompt_terms.append(jnp.stack([prompt_dkey, prompt_dvalue], axis=2))
    d_query = query_grad.astype(jnp.bfloat16)
    d_key = product("kgtu,tkgh->ukh", self_grad, queries).astype(jnp.bfloat16)
    d_value = product("kgtu,tkgh->ukh", self_rounded, dout).astype(jnp.bfloat16)
    d_packed = jnp.concatenate([d_query, d_key[:, :, None], d_value[:, :, None]], axis=2)
    return (attended, d_packed, jnp.stack(prompt_terms, axis=0))


def local(projected, grad_output, prompt_cache, segment_ids, segment_prompt):
    group_size = HEADS // KV_HEADS
    packed, dout = (
        lax.all_to_all(projected, "head", split_axis=1, concat_axis=0, tiled=True),
        lax.all_to_all(grad_output, "head", split_axis=1, concat_axis=0, tiled=True),
    )
    row_count = packed.shape[0]
    kv_local = packed.shape[1] // ((group_size + 2) * HEAD_DIM)
    packed = packed.reshape(row_count, kv_local, group_size + 2, HEAD_DIM)
    dout = dout.reshape(row_count, kv_local, group_size, HEAD_DIM)
    cache_slots = []
    for distance in range(-REACH, REACH + 1):
        if distance == 0:
            cache_slots.append(prompt_cache)
        else:
            cache_slots.append(passed_along(prompt_cache, "dp", -distance))
    stacked = jnp.stack(cache_slots).reshape(2 * REACH + 1, PROMPT_LEN, kv_local, 2, HEAD_DIM)
    dp_index = lax.axis_index("dp")
    dp_count = lax.axis_size("dp")
    slot_index = (segment_prompt[0] - dp_index + dp_count + REACH) % dp_count
    prompt_blocks = stacked[slot_index]
    attended, d_packed, prompt_terms = attend(
        packed[:, :, :group_size],
        packed[:, :, group_size],
        packed[:, :, group_size + 1],
        dout,
        segment_ids[0],
        prompt_blocks,
    )
    slot_terms = (
        jnp.zeros((2 * REACH + 1, PROMPT_LEN, kv_local, 2, HEAD_DIM), jnp.float32)
        .at[slot_index]
        .add(prompt_terms)
    )
    slot_terms = slot_terms.reshape(2 * REACH + 1, PROMPT_LEN, kv_local * 2 * HEAD_DIM)
    returned = slot_terms[REACH]
    for distance in range(-REACH, REACH + 1):
        if distance != 0:
            returned = returned + passed_along(slot_terms[distance + REACH], "dp", distance)
    attention_out, grad_projected = (
        lax.all_to_all(
            attended.reshape(row_count, -1), "head", split_axis=0, concat_axis=1, tiled=True
        ),
        lax.all_to_all(
            d_packed.reshape(row_count, -1), "head", split_axis=0, concat_axis=1, tiled=True
        ),
    )
    return (attention_out, grad_projected, returned.astype(jnp.bfloat16))


def solution(mesh):
    return jax.shard_map(
        local,
        mesh=mesh,
        in_specs=(
            P(("dp", "head"), None),
            P(("dp", "head"), None),
            P("dp", "head"),
            P("dp", None),
            P("dp", None),
        ),
        out_specs=(P(("dp", "head"), None), P(("dp", "head"), None), P("dp", "head")),
        check_vma=False,
    )
```

profile of v0, /device:TPU:1, one launch (start us, length us, event | category | flops | bytes accessed | tf_op | source)
XLA Modules:
  0.0 231.4 jit_solution(470082943162486640)
XLA Ops:
  1.7 13.7 %collective-permute-start.7 = (bf16[512,256]{0,1:T(8,128)(2,1)S(1)}, bf16[512,256]{0,1:T(8,128)(2,1)S(1)}, u32[]{:S(2)}, u32[]{:S(2)}) collective-permute-start(bf16[512,256]{0,1:T(8,128)(2,1)S(1)} %copy.41), channel_id=1, source_target_pairs={{32,0},{40,8},{48,16},{56,24},{64,32},{72,40},{80,48},{88,56},{96,... | collective-permute-start | bytes 786440 | tf_op jit(solution)/shard_map/ppermute | solution.py:18
  15.4 3.0 %collective-permute-start.6 = (bf16[512,256]{0,1:T(8,128)(2,1)S(1)}, bf16[512,256]{0,1:T(8,128)(2,1)S(1)}, u32[]{:S(2)}, u32[]{:S(2)}) collective-permute-start(bf16[512,256]{0,1:T(8,128)(2,1)S(1)} %copy.41), channel_id=1, source_target_pairs={{24,0},{32,8},{40,16},{48,24},{56,32},{64,40},{72,48},{80,56},{88,... | collective-permute-start | bytes 786440 | tf_op jit(solution)/shard_map/ppermute | solution.py:18
  18.4 3.1 %collective-permute-start.2 = (bf16[512,256]{0,1:T(8,128)(2,1)S(1)}, bf16[512,256]{0,1:T(8,128)(2,1)S(1)}, u32[]{:S(2)}, u32[]{:S(2)}) collective-permute-start(bf16[512,256]{0,1:T(8,128)(2,1)S(1)} %copy.41), channel_id=1, source_target_pairs={{496,0},{504,8},{0,16},{8,24},{16,32},{24,40},{32,48},{40,56},{48,... | collective-permute-start | bytes 786440 | tf_op jit(solution)/shard_map/ppermute | solution.py:18
  21.6 3.7 %collective-permute-start.1 = (bf16[512,256]{0,1:T(8,128)(2,1)S(1)}, bf16[512,256]{0,1:T(8,128)(2,1)S(1)}, u32[]{:S(2)}, u32[]{:S(2)}) collective-permute-start(bf16[512,256]{0,1:T(8,128)(2,1)S(1)} %copy.41), channel_id=1, source_target_pairs={{488,0},{496,8},{504,16},{0,24},{8,32},{16,40},{24,48},{32,56},{40... | collective-permute-start | bytes 786440 | tf_op jit(solution)/shard_map/ppermute | solution.py:18
  28.8 6.8 %all-to-all-start.2 = ((bf16[16,8,640]{2,0,1:T(8,128)(2,1)}), bf16[16,8,640]{2,0,1:T(8,128)(2,1)S(1)}, u32[]{:S(2)}, u32[]{:S(2)}) async-start(bf16[16,8,640]{2,0,1:T(8,128)(2,1)} %bitcast.571), calls=%async_computation.2 | async-start | bytes 327680 | tf_op jit(solution)/shard_map/all_to_all | solution.py:121
  43.8 5.7 %collective-permute-done = bf16[512,256]{0,1:T(8,128)(2,1)S(1)} collective-permute-done((bf16[512,256]{0,1:T(8,128)(2,1)S(1)}, bf16[512,256]{0,1:T(8,128)(2,1)S(1)}, u32[]{:S(2)}, u32[]{:S(2)}) %collective-permute-start) | collective-permute-done | bytes 262176 | tf_op jit(solution)/shard_map/ppermute | solution.py:18
  49.5 5.5 %collective-permute-start.3 = (bf16[512,256]{0,1:T(8,128)(2,1)S(1)}, bf16[512,256]{0,1:T(8,128)(2,1)S(1)}, u32[]{:S(2)}, u32[]{:S(2)}) collective-permute-start(bf16[512,256]{0,1:T(8,128)(2,1)S(1)} %copy.41), channel_id=1, source_target_pairs={{504,0},{0,8},{8,16},{16,24},{24,32},{32,40},{40,48},{48,56},{56,6... | collective-permute-start | bytes 786440 | tf_op jit(solution)/shard_map/ppermute | solution.py:18
  55.9 3.4 %collective-permute-start.5 = (bf16[512,256]{0,1:T(8,128)(2,1)S(1)}, bf16[512,256]{0,1:T(8,128)(2,1)S(1)}, u32[]{:S(2)}, u32[]{:S(2)}) collective-permute-start(bf16[512,256]{0,1:T(8,128)(2,1)S(1)} %copy.41), channel_id=1, source_target_pairs={{16,0},{24,8},{32,16},{40,24},{48,32},{56,40},{64,48},{72,56},{80,... | collective-permute-start | bytes 786440 | tf_op jit(solution)/shard_map/ppermute | solution.py:18
  65.1 2.4 %collective-permute-done.4 = bf16[512,256]{0,1:T(8,128)(2,1)S(1)} collective-permute-done((bf16[512,256]{0,1:T(8,128)(2,1)S(1)}, bf16[512,256]{0,1:T(8,128)(2,1)S(1)}, u32[]{:S(2)}, u32[]{:S(2)}) %collective-permute-start.4) | collective-permute-done | bytes 262176 | tf_op jit(solution)/shard_map/ppermute | solution.py:18
  68.4 6.8 %all-to-all-start = ((bf16[16,8,896]{2,0,1:T(8,128)(2,1)}), bf16[16,8,896]{2,0,1:T(8,128)(2,1)S(1)}, u32[]{:S(2)}, u32[]{:S(2)}) async-start(bf16[16,8,896]{2,0,1:T(8,128)(2,1)} %bitcast.570), calls=%async_computation | async-start | bytes 458752 | tf_op jit(solution)/shard_map/all_to_all | solution.py:120
  77.7 2.4 %gather_fusion = bf16[4,512,2,128]{3,1,2,0:T(8,128)(2,1)S(1)} fusion(bf16[9,512,2,128]{3,1,2,0:T(8,128)(2,1)} %bitcast.597, s32[1024]{0:T(1024)S(1)} %pad_clamp_fusion), kind=kCustom, calls=%fused_computation | custom fusion | bytes 2097168 | tf_op jit(solution)/shard_map/gather | solution.py:137
  82.1 3.6 %all-to-all-done = bf16[16,8,896]{2,0,1:T(8,128)(2,1)S(1)} async-done(((bf16[16,8,896]{2,0,1:T(8,128)(2,1)}), bf16[16,8,896]{2,0,1:T(8,128)(2,1)S(1)}, u32[]{:S(2)}, u32[]{:S(2)}) %all-to-all-start) | async-done | bytes 229408 | tf_op jit(solution)/shard_map/all_to_all | solution.py:120
  125.2 4.2 %all-to-all-start.1 = ((bf16[8,16,640]{2,1,0:T(8,128)(2,1)}), bf16[8,16,640]{2,1,0:T(8,128)(2,1)}, u32[]{:S(2)}, u32[]{:S(2)}) async-start(bf16[8,16,640]{2,1,0:T(8,128)(2,1)} %all_to_all.55), calls=%async_computation.1 | async-start | bytes 327680 | tf_op jit(solution)/shard_map/all_to_all | solution.py:157
  136.1 2.7 %broadcast.170 = f32[9,512,2,128]{3,1,2,0:T(8,128)} broadcast(f32[]{:T(128)} %constant.59.clone.1), dimensions={} | broadcast | bytes 4718596 | tf_op jit(solution)/shard_map/broadcast_in_dim | solution.py:147
  138.7 4.2 %scatter_fusion = f32[9,512,2,128]{3,1,2,0:T(8,128)} fusion(f32[9,512,2,128]{3,1,2,0:T(8,128)} %broadcast.170, s32[4]{0:T(128)S(1)} %fusion.156, f32[4,512,2,128]{3,1,2,0:T(8,128)S(1)} %copy.74), kind=kCustom, calls=%fused_computation.1 | custom fusion | flops 524288 | bytes 6291472 | tf_op jit(solution)/shard_map/scatter-add | solution.py:149
  142.9 4.0 %fusion.159 = (f32[1,512,2,128]{3,1,2,0:T(8,128)S(1)}, f32[1,512,2,128]{3,1,2,0:T(8,128)}, f32[1,512,2,128]{3,1,2,0:T(8,128)}, f32[1,512,2,128]{3,1,2,0:T(8,128)...) fusion(f32[9,512,2,128]{3,1,2,0:T(8,128)} %scatter_fusion), kind=kLoop, calls=%fused_computation.260 | loop fusion | bytes 9437184 | tf_op jit(solution)/shard_map/slice | solution.py:152
  155.1 7.6 %collective-permute-start.8 = (f32[512,256]{0,1:T(8,128)}, f32[512,256]{0,1:T(8,128)}, u32[]{:S(2)}, u32[]{:S(2)}) collective-permute-start(f32[512,256]{0,1:T(8,128)} %bitcast.602), channel_id=1, source_target_pairs={{32,0},{40,8},{48,16},{56,24},{64,32},{72,40},{80,48},{88,56},{96,... | collective-permute-start | bytes 1572872 | tf_op jit(solution)/shard_map/ppermute | solution.py:18
  162.6 2.9 %collective-permute-start.9 = (f32[512,256]{0,1:T(8,128)}, f32[512,256]{0,1:T(8,128)}, u32[]{:S(2)}, u32[]{:S(2)}) collective-permute-start(f32[512,256]{0,1:T(8,128)} %bitcast.601), channel_id=1, source_target_pairs={{24,0},{32,8},{40,16},{48,24},{56,32},{64,40},{72,48},{80,56},{88,... | collective-permute-start | bytes 1572872 | tf_op jit(solution)/shard_map/ppermute | solution.py:18
  179.7 2.3 collective-permute-start.11
  183.6 4.3 %collective-permute-start.12 = (f32[512,256]{0,1:T(8,128)}, f32[512,256]{0,1:T(8,128)S(1)}, u32[]{:S(2)}, u32[]{:S(2)}) collective-permute-start(f32[512,256]{0,1:T(8,128)} %bitcast.600), channel_id=1, source_target_pairs={{504,0},{0,8},{8,16},{16,24},{24,32},{32,40},{40,48},{48,56},{56,6... | collective-permute-start | bytes 1572872 | tf_op jit(solution)/shard_map/ppermute | solution.py:18
  189.9 11.8 %collective-permute-done.9 = f32[512,256]{0,1:T(8,128)} collective-permute-done((f32[512,256]{0,1:T(8,128)}, f32[512,256]{0,1:T(8,128)}, u32[]{:S(2)}, u32[]{:S(2)}) %collective-permute-start.9) | collective-permute-done | bytes 524320 | tf_op jit(solution)/shard_map/ppermute | solution.py:18
  205.3 6.3 %all-to-all-start.3 = ((bf16[8,16,896]{2,1,0:T(8,128)(2,1)}), bf16[8,16,896]{2,1,0:T(8,128)(2,1)S(1)}, u32[]{:S(2)}, u32[]{:S(2)}) async-start(bf16[8,16,896]{2,1,0:T(8,128)(2,1)} %all_to_all.62), calls=%async_computation.3 | async-start | bytes 458752 | tf_op jit(solution)/shard_map/all_to_all | solution.py:160
  213.4 8.0 %all-to-all-done.3 = bf16[8,16,896]{2,1,0:T(8,128)(2,1)S(1)} async-done(((bf16[8,16,896]{2,1,0:T(8,128)(2,1)}), bf16[8,16,896]{2,1,0:T(8,128)(2,1)S(1)}, u32[]{:S(2)}, u32[]{:S(2)}) %all-to-all-start.3) | async-done | bytes 229408 | tf_op jit(solution)/shard_map/all_to_all | solution.py:160
  222.9 5.4 %collective-permute-done.14 = f32[512,256]{0,1:T(8,128)} collective-permute-done((f32[512,256]{0,1:T(8,128)}, f32[512,256]{0,1:T(8,128)}, u32[]{:S(2)}, u32[]{:S(2)}) %collective-permute-start.14) | collective-permute-done | bytes 524320 | tf_op jit(solution)/shard_map/ppermute | solution.py:18
  (203 shorter events, 103.7 us)
Async XLA Ops:
  1.7 74.2 %collective-permute-start.7 = (bf16[512,256]{0,1:T(8,128)(2,1)S(1)}, bf16[512,256]{0,1:T(8,128)(2,1)S(1)}, u32[]{:S(2)}, u32[]{:S(2)}) collective-permute-start(bf16[512,256]{0,1:T(8,128)(2,1)S(1)} %copy.41), channel_id=1, source_target_pairs={{32,0},{40,8},{48,16},{56,24},{64,32},{72,40},{80,48},{88,56},{96,... | collective-permute-start | bytes 786440 | tf_op jit(solution)/shard_map/ppermute | solution.py:18
  15.4 60.7 %collective-permute-start.6 = (bf16[512,256]{0,1:T(8,128)(2,1)S(1)}, bf16[512,256]{0,1:T(8,128)(2,1)S(1)}, u32[]{:S(2)}, u32[]{:S(2)}) collective-permute-start(bf16[512,256]{0,1:T(8,128)(2,1)S(1)} %copy.41), channel_id=1, source_target_pairs={{24,0},{32,8},{40,16},{48,24},{56,32},{64,40},{72,48},{80,56},{88,... | collective-permute-start | bytes 786440 | tf_op jit(solution)/shard_map/ppermute | solution.py:18
  18.4 37.5 %collective-permute-start.2 = (bf16[512,256]{0,1:T(8,128)(2,1)S(1)}, bf16[512,256]{0,1:T(8,128)(2,1)S(1)}, u32[]{:S(2)}, u32[]{:S(2)}) collective-permute-start(bf16[512,256]{0,1:T(8,128)(2,1)S(1)} %copy.41), channel_id=1, source_target_pairs={{496,0},{504,8},{0,16},{8,24},{16,32},{24,40},{32,48},{40,56},{48,... | collective-permute-start | bytes 786440 | tf_op jit(solution)/shard_map/ppermute | solution.py:18
  21.6 37.9 %collective-permute-start.1 = (bf16[512,256]{0,1:T(8,128)(2,1)S(1)}, bf16[512,256]{0,1:T(8,128)(2,1)S(1)}, u32[]{:S(2)}, u32[]{:S(2)}) collective-permute-start(bf16[512,256]{0,1:T(8,128)(2,1)S(1)} %copy.41), channel_id=1, source_target_pairs={{488,0},{496,8},{504,16},{0,24},{8,32},{16,40},{24,48},{32,56},{40... | collective-permute-start | bytes 786440 | tf_op jit(solution)/shard_map/ppermute | solution.py:18
  25.3 24.2 %collective-permute-start = (bf16[512,256]{0,1:T(8,128)(2,1)S(1)}, bf16[512,256]{0,1:T(8,128)(2,1)S(1)}, u32[]{:S(2)}, u32[]{:S(2)}) collective-permute-start(bf16[512,256]{0,1:T(8,128)(2,1)S(1)} %copy.41), channel_id=1, source_target_pairs={{480,0},{488,8},{496,16},{504,24},{0,32},{8,40},{16,48},{24,56},{3... | collective-permute-start | bytes 786440 | tf_op jit(solution)/shard_map/ppermute | solution.py:18
  28.8 39.6 %all-to-all-start.2 = ((bf16[16,8,640]{2,0,1:T(8,128)(2,1)}), bf16[16,8,640]{2,0,1:T(8,128)(2,1)S(1)}, u32[]{:S(2)}, u32[]{:S(2)}) async-start(bf16[16,8,640]{2,0,1:T(8,128)(2,1)} %bitcast.571), calls=%async_computation.2 | async-start | bytes 327680 | tf_op jit(solution)/shard_map/all_to_all | solution.py:121
  49.5 13.5 %collective-permute-start.3 = (bf16[512,256]{0,1:T(8,128)(2,1)S(1)}, bf16[512,256]{0,1:T(8,128)(2,1)S(1)}, u32[]{:S(2)}, u32[]{:S(2)}) collective-permute-start(bf16[512,256]{0,1:T(8,128)(2,1)S(1)} %copy.41), channel_id=1, source_target_pairs={{504,0},{0,8},{8,16},{16,24},{24,32},{32,40},{40,48},{48,56},{56,6... | collective-permute-start | bytes 786440 | tf_op jit(solution)/shard_map/ppermute | solution.py:18
  55.9 9.0 %collective-permute-start.5 = (bf16[512,256]{0,1:T(8,128)(2,1)S(1)}, bf16[512,256]{0,1:T(8,128)(2,1)S(1)}, u32[]{:S(2)}, u32[]{:S(2)}) collective-permute-start(bf16[512,256]{0,1:T(8,128)(2,1)S(1)} %copy.41), channel_id=1, source_target_pairs={{16,0},{24,8},{32,16},{40,24},{48,32},{56,40},{64,48},{72,56},{80,... | collective-permute-start | bytes 786440 | tf_op jit(solution)/shard_map/ppermute | solution.py:18
  59.5 8.0 %collective-permute-start.4 = (bf16[512,256]{0,1:T(8,128)(2,1)S(1)}, bf16[512,256]{0,1:T(8,128)(2,1)S(1)}, u32[]{:S(2)}, u32[]{:S(2)}) collective-permute-start(bf16[512,256]{0,1:T(8,128)(2,1)S(1)} %copy.41), channel_id=1, source_target_pairs={{8,0},{16,8},{24,16},{32,24},{40,32},{48,40},{56,48},{64,56},{72,6... | collective-permute-start | bytes 786440 | tf_op jit(solution)/shard_map/ppermute | solution.py:18
  68.4 17.3 %all-to-all-start = ((bf16[16,8,896]{2,0,1:T(8,128)(2,1)}), bf16[16,8,896]{2,0,1:T(8,128)(2,1)S(1)}, u32[]{:S(2)}, u32[]{:S(2)}) async-start(bf16[16,8,896]{2,0,1:T(8,128)(2,1)} %bitcast.570), calls=%async_computation | async-start | bytes 458752 | tf_op jit(solution)/shard_map/all_to_all | solution.py:120
  125.2 80.2 %all-to-all-start.1 = ((bf16[8,16,640]{2,1,0:T(8,128)(2,1)}), bf16[8,16,640]{2,1,0:T(8,128)(2,1)}, u32[]{:S(2)}, u32[]{:S(2)}) async-start(bf16[8,16,640]{2,1,0:T(8,128)(2,1)} %all_to_all.55), calls=%async_computation.1 | async-start | bytes 327680 | tf_op jit(solution)/shard_map/all_to_all | solution.py:157
  146.9 18.6 %copy-start.2 = (f32[128,1,5,128]{3,0,2,1:T(8,128)S(1)}, f32[128,1,5,128]{3,0,2,1:T(8,128)}, u32[]{:S(2)}) copy-start(f32[128,1,5,128]{3,0,2,1:T(8,128)} %copy-done.1) | copy-start | bytes 983044
  146.9 23.6 %copy-start.9 = (f32[1,5,128,128]{2,3,1,0:T(8,128)S(1)}, f32[1,5,128,128]{2,3,1,0:T(8,128)}, u32[]{:S(2)}) copy-start(f32[1,5,128,128]{2,3,1,0:T(8,128)} %get-tuple-element.55) | copy-start | bytes 983044
  153.1 30.5 %collective-permute-start.15 = (f32[512,256]{0,1:T(8,128)}, f32[512,256]{0,1:T(8,128)}, u32[]{:S(2)}, u32[]{:S(2)}) collective-permute-start(f32[512,256]{0,1:T(8,128)} %bitcast.603), channel_id=1, source_target_pairs={{480,0},{488,8},{496,16},{504,24},{0,32},{8,40},{16,48},{24,56},{3... | collective-permute-start | bytes 1572872 | tf_op jit(solution)/shard_map/ppermute | solution.py:18
  155.1 32.9 %collective-permute-start.8 = (f32[512,256]{0,1:T(8,128)}, f32[512,256]{0,1:T(8,128)}, u32[]{:S(2)}, u32[]{:S(2)}) collective-permute-start(f32[512,256]{0,1:T(8,128)} %bitcast.602), channel_id=1, source_target_pairs={{32,0},{40,8},{48,16},{56,24},{64,32},{72,40},{80,48},{88,56},{96,... | collective-permute-start | bytes 1572872 | tf_op jit(solution)/shard_map/ppermute | solution.py:18
  162.6 39.1 %collective-permute-start.9 = (f32[512,256]{0,1:T(8,128)}, f32[512,256]{0,1:T(8,128)}, u32[]{:S(2)}, u32[]{:S(2)}) collective-permute-start(f32[512,256]{0,1:T(8,128)} %bitcast.601), channel_id=1, source_target_pairs={{24,0},{32,8},{40,16},{48,24},{56,32},{64,40},{72,48},{80,56},{88,... | collective-permute-start | bytes 1572872 | tf_op jit(solution)/shard_map/ppermute | solution.py:18
  173.8 29.8 %copy-start.19 = (bf16[5,128,128]{1,2,0:T(8,128)(2,1)S(1)}, bf16[5,128,128]{1,2,0:T(8,128)(2,1)}, u32[]{:S(2)}) copy-start(bf16[5,128,128]{1,2,0:T(8,128)(2,1)} %copy-done.18) | copy-start | bytes 491524
  173.8 30.0 %copy-start.20 = (f32[64,1,5,128]{3,0,2,1:T(8,128)S(1)}, f32[64,1,5,128]{3,0,2,1:T(8,128)}, u32[]{:S(2)}) copy-start(f32[64,1,5,128]{3,0,2,1:T(8,128)} %fusion.45) | copy-start | bytes 491524
  177.8 44.3 %collective-permute-start.10 = (f32[512,256]{0,1:T(8,128)}, f32[512,256]{0,1:T(8,128)S(1)}, u32[]{:S(2)}, u32[]{:S(2)}) collective-permute-start(f32[512,256]{0,1:T(8,128)} %bitcast.200), channel_id=1, source_target_pairs={{16,0},{24,8},{32,16},{40,24},{48,32},{56,40},{64,48},{72,56},{80,... | collective-permute-start | bytes 1572872 | tf_op jit(solution)/shard_map/ppermute | solution.py:18
  179.7 42.4 %collective-permute-start.11 = (f32[512,256]{0,1:T(8,128)}, f32[512,256]{0,1:T(8,128)S(1)}, u32[]{:S(2)}, u32[]{:S(2)}) collective-permute-start(f32[512,256]{0,1:T(8,128)} %bitcast.201), channel_id=1, source_target_pairs={{8,0},{16,8},{24,16},{32,24},{40,32},{48,40},{56,48},{64,56},{72,6... | collective-permute-start | bytes 1572872 | tf_op jit(solution)/shard_map/ppermute | solution.py:18
  183.6 38.5 %collective-permute-start.12 = (f32[512,256]{0,1:T(8,128)}, f32[512,256]{0,1:T(8,128)S(1)}, u32[]{:S(2)}, u32[]{:S(2)}) collective-permute-start(f32[512,256]{0,1:T(8,128)} %bitcast.600), channel_id=1, source_target_pairs={{504,0},{0,8},{8,16},{16,24},{24,32},{32,40},{40,48},{48,56},{56,6... | collective-permute-start | bytes 1572872 | tf_op jit(solution)/shard_map/ppermute | solution.py:18
  188.0 34.2 %collective-permute-start.13 = (f32[512,256]{0,1:T(8,128)}, f32[512,256]{0,1:T(8,128)}, u32[]{:S(2)}, u32[]{:S(2)}) collective-permute-start(f32[512,256]{0,1:T(8,128)} %bitcast.599), channel_id=1, source_target_pairs={{496,0},{504,8},{0,16},{8,24},{16,32},{24,40},{32,48},{40,56},{48,... | collective-permute-start | bytes 1572872 | tf_op jit(solution)/shard_map/ppermute | solution.py:18
  201.7 26.6 %collective-permute-start.14 = (f32[512,256]{0,1:T(8,128)}, f32[512,256]{0,1:T(8,128)}, u32[]{:S(2)}, u32[]{:S(2)}) collective-permute-start(f32[512,256]{0,1:T(8,128)} %bitcast.598), channel_id=1, source_target_pairs={{488,0},{496,8},{504,16},{0,24},{8,32},{16,40},{24,48},{32,56},{40... | collective-permute-start | bytes 1572872 | tf_op jit(solution)/shard_map/ppermute | solution.py:18
  205.3 16.1 %all-to-all-start.3 = ((bf16[8,16,896]{2,1,0:T(8,128)(2,1)}), bf16[8,16,896]{2,1,0:T(8,128)(2,1)S(1)}, u32[]{:S(2)}, u32[]{:S(2)}) async-start(bf16[8,16,896]{2,1,0:T(8,128)(2,1)} %all_to_all.62), calls=%async_computation.3 | async-start | bytes 458752 | tf_op jit(solution)/shard_map/all_to_all | solution.py:160
  (26 other events, 74.2 us)
where the time goes:
time: 233 us; the launch traced here: 231 us
  starting transfers between devices  85.1 us (37%)
  local copies, waits for them, and re-layouts  57.9 us (25%)
  waiting for transfers between devices  38.7 us (17%)
  matrix products  27 us (12%)
  other arithmetic  18.7 us (8%)
  between operations  3.97 us (2%)
    ppermute x16, starting transfers between devices, passed_along(): return lax.ppermute(block, axis, route)  61 us
    ppermute x16, waiting for transfers between devices, passed_along(): return lax.ppermute(block, axis, route)  27.1 us
    dot_general x30, matrix products, product(): return jnp.einsum(form, left, right, preferred_element_type=jnp.float32)  27 us
    slice x8, local copies, waits for them, and re-layouts, local(): slot_terms[distance + REACH]  12.2 us
    unnamed x71, local copies, waits for them, and re-layouts  10.4 us
    all_to_all x1, waiting for transfers between devices, local(): lax.all_to_all(d_packed.reshape(row_count, -1), 'head', split_axis=0, con...  7.99 us
    add x4, local copies, waits for them, and re-layouts, attend(): attended + place(product('kgtl,lkh->tkgh', rounded, prompt_values[segment...  7.02 us
    all_to_all x1, starting transfers between devices, local(): lax.all_to_all(projected, 'head', split_axis=1, concat_axis=0, tiled=True)  6.82 us
  transfers between devices with their start and end apart: 20, of which 8 were waited for; matrix products, arithmetic and copies ran while one was open for 25% of the time, Pallas kernels for 0%

commit v1 on v0

v1 whole, which is shorter than its diff:
```python
import jax
import jax.numpy as jnp
from jax import lax
from jax.experimental import pallas as pl
from jax.experimental.pallas import tpu as pltpu
from jax.sharding import PartitionSpec as P

HEADS = 40
KV_HEADS = 8
HEAD_DIM = 128
GROUP = HEADS // KV_HEADS
TOK_DEV = 128
PROMPT_LEN = 512
SEGS = 4
REACH = 4
SEG_MOST = 64
N_DP = 64
CHIPS = N_DP // 2
N_HEAD = 8
ROWS = TOK_DEV // N_HEAD
PACK = (GROUP + 2) * HEAD_DIM
OUT = GROUP * HEAD_DIM
STACK = GROUP * SEG_MOST
KEYS = PROMPT_LEN + HEAD_DIM
SCALE = HEAD_DIM**-0.5
LOG2E = 1.4426950408889634
MESH = pl.DeviceIdType.MESH
F32 = jnp.float32
BF16 = jnp.bfloat16
COPIES = 72


def dot(left, right, contract):
    return lax.dot_general(left, right, (contract, ((), ())), preferred_element_type=F32)


def heads_down(block):
    return jnp.concatenate([block[:, g * HEAD_DIM : (g + 1) * HEAD_DIM] for g in range(GROUP)], axis=0)


def kernel(
    ids_ref, owner_ref, proj, gout, cache,
    att_out, dproj_out, dcache_out,
    pk, dk, keys, values, win_q, win_kv, win_d, prob, term, win_o, win_g, att_send, dproj_send,
    sib_send, sib_recv, far_send, far_recv, near_send, near_recv,
    local_sem, send_sem, recv_sem,
):
    dp = lax.axis_index("dp")
    head = lax.axis_index("head")
    chip = dp // 2
    core = lax.rem(dp, 2)
    sibling = (dp + 1 - 2 * core, head)
    right = (lax.rem(chip + 1, CHIPS) * 2 + core, head)
    left = (lax.rem(chip + CHIPS - 1, CHIPS) * 2 + core, head)
    peers = [lax.rem(head + j, N_HEAD) for j in range(1, N_HEAD)]
    used = [0]
    kv = (keys, values)

    def send(src, dst, device):
        i = used[0]
        used[0] += 1
        copy = pltpu.make_async_remote_copy(
            src_ref=src, dst_ref=dst, send_sem=send_sem.at[i], recv_sem=recv_sem.at[i],
            device_id=device, device_id_type=MESH,
        )
        copy.start()
        return copy

    def columns(index, width):
        return pl.ds(pl.multiple_of(index * width, HEAD_DIM), width)

    local = [
        pltpu.make_async_copy(cache.at[:, pl.ds(w * HEAD_DIM, HEAD_DIM)], kv[w].at[2], local_sem.at[w])
        for w in range(2)
    ]
    local.append(pltpu.make_async_copy(proj.at[:, columns(head, PACK)], pk.at[head], local_sem.at[2]))
    local.append(pltpu.make_async_copy(gout.at[:, columns(head, OUT)], dk.at[head], local_sem.at[3]))
    for copy in local:
        copy.start()
    barrier = pltpu.get_barrier_semaphore()
    partners = [sibling, right, left] + [(dp, p) for p in peers]
    for partner in partners:
        pl.semaphore_signal(barrier, inc=1, device_id=partner, device_id_type=MESH)

    ids = ids_ref[...]
    position = lax.broadcasted_iota(jnp.int32, (1, TOK_DEV), 1)
    first = jnp.zeros((1, TOK_DEV), jnp.int32)
    for s in range(SEGS):
        before = jnp.sum((ids < s).astype(jnp.int32), axis=1, keepdims=True)
        first = first + jnp.where(ids == s, before, 0)
    row = (ids * SEG_MOST + position - first).astype(F32)
    rows = lax.broadcasted_iota(jnp.int32, (SEGS * SEG_MOST, TOK_DEV), 0).astype(F32)
    pick = (jnp.broadcast_to(row, rows.shape) == rows).astype(BF16)
    row_t = jnp.transpose(jnp.broadcast_to(row, (TOK_DEV, TOK_DEV)))
    cols = lax.broadcasted_iota(jnp.int32, (TOK_DEV, SEGS * SEG_MOST), 1).astype(F32)
    unpick = (jnp.concatenate([row_t, row_t], axis=1) == cols).astype(BF16)

    offsets, slots = [], []
    for s in range(SEGS):
        offset = lax.rem(owner_ref[0, s] - dp + N_DP + REACH, N_DP) - REACH
        odd = lax.rem(offset + 8, 2)
        away = jnp.where(odd == 1, offset - 1 + 2 * core, offset) // 2
        slot = jnp.where(
            odd == 0, jnp.clip(away, -2, 2) + 2,
            jnp.where(away == 0, 5, jnp.where(away == 1, 6, jnp.where(away == -1, 7, 8))),
        )
        offsets.append(offset)
        slots.append(slot)

    def slot_of(s):
        return jnp.where(s == 0, slots[0], jnp.where(s == 1, slots[1], jnp.where(s == 2, slots[2], slots[3])))

    for w in range(2):
        local[w].wait()
    pl.semaphore_wait(barrier, len(partners))

    pending = []
    near, far, sib = [None, None], [None, None], [[], []]
    a2a = [[], []]
    near[0] = [send(kv[0].at[2], kv[0].at[1], right), send(kv[0].at[2], kv[0].at[3], left)]
    sib[0].append(send(kv[0].at[2], kv[0].at[5], sibling))
    for p in peers:
        a2a[0].append(send(proj.at[:, columns(p, PACK)], pk.at[head], (dp, p)))
    near[1] = [send(kv[1].at[2], kv[1].at[1], right), send(kv[1].at[2], kv[1].at[3], left)]
    sib[1].append(send(kv[1].at[2], kv[1].at[5], sibling))
    for p in peers:
        a2a[1].append(send(gout.at[:, columns(p, OUT)], dk.at[head], (dp, p)))
    for w in range(2):
        near[w][0].wait_recv()
        f0 = send(kv[w].at[1], kv[w].at[0], right)
        sib[w].append(send(kv[w].at[1], kv[w].at[7], sibling))
        near[w][1].wait_recv()
        f1 = send(kv[w].at[3], kv[w].at[4], left)
        sib[w].append(send(kv[w].at[3], kv[w].at[6], sibling))
        far[w] = [f0, f1]

    def spread(picked, window):
        for g in range(GROUP):
            part = picked[:, g * HEAD_DIM : (g + 1) * HEAD_DIM]
            window[:, g] = part.reshape(SEGS, SEG_MOST, HEAD_DIM)

    local[2].wait()
    local[3].wait()
    for copy in a2a[0]:
        copy.wait_recv()
    picked = dot(pick, pk[...].reshape(TOK_DEV, PACK), ((1,), (0,))).astype(BF16)
    spread(picked, win_q)
    for w in range(2):
        own = picked[:, OUT + w * HEAD_DIM : OUT + (w + 1) * HEAD_DIM].reshape(SEGS, SEG_MOST, HEAD_DIM)
        win_kv[w] = jnp.concatenate([own, jnp.zeros_like(own)], axis=1)
    for copy in a2a[1]:
        copy.wait_recv()
    picked = dot(pick, dk[...].reshape(TOK_DEV, OUT), ((1,), (0,))).astype(BF16)
    spread(picked, win_d)

    def arrived(w):
        for copy in far[w]:
            copy.wait_recv()
        sib[w].append(send(kv[w].at[4 - 4 * core], kv[w].at[8], sibling))
        for copy in sib[w]:
            copy.wait_recv()

    def all_rows(w, s):
        return jnp.concatenate([kv[w][slot_of(s)], win_kv[w, s]], axis=0)

    key_at = lax.broadcasted_iota(jnp.int32, (STACK, HEAD_DIM), 1)
    row_at = lax.rem(lax.broadcasted_iota(jnp.int32, (STACK, HEAD_DIM), 0), SEG_MOST)

    def weigh(s, carry):
        queries = win_q[s].reshape(STACK, HEAD_DIM)
        dout = win_d[s].reshape(STACK, HEAD_DIM)
        scores = dot(queries, all_rows(0, s), ((1,), (1,)))
        own = jnp.where(key_at <= row_at, scores[:, PROMPT_LEN:], -1e30)
        scores = jnp.concatenate([scores[:, :PROMPT_LEN], own], axis=1)
        top = jnp.max(scores, axis=1, keepdims=True)
        expo = jnp.exp2((scores - top) * (SCALE * LOG2E))
        weights = expo * (1.0 / jnp.sum(expo, axis=1, keepdims=True))
        prob[s] = weights
        dvalue = dot(weights.astype(BF16), dout, ((0,), (0,)))
        term[1, s] = dvalue[:PROMPT_LEN]
        win_g[s, GROUP + 1] = dvalue[PROMPT_LEN : PROMPT_LEN + SEG_MOST].astype(BF16)
        return carry

    def attend(s, carry):
        out = dot(prob[s].astype(BF16), all_rows(1, s), ((1,), (0,))).astype(BF16)
        win_o[s] = out.reshape(GROUP, SEG_MOST, HEAD_DIM)
        return carry

    def differentiate(s, carry):
        queries = win_q[s].reshape(STACK, HEAD_DIM)
        dout = win_d[s].reshape(STACK, HEAD_DIM)
        out = win_o[s].reshape(STACK, HEAD_DIM)
        delta = jnp.sum(dout.astype(F32) * out.astype(F32), axis=1, keepdims=True)
        dweight = dot(dout, all_rows(1, s), ((1,), (1,)))
        dscore = (prob[s] * (dweight - delta) * SCALE).astype(BF16)
        dquery = dot(dscore, all_rows(0, s), ((1,), (0,))).astype(BF16)
        win_g[s, :GROUP] = dquery.reshape(GROUP, SEG_MOST, HEAD_DIM)
        dkey = dot(dscore, queries, ((0,), (0,)))
        term[0, s] = dkey[:PROMPT_LEN]
        win_g[s, GROUP] = dkey[PROMPT_LEN : PROMPT_LEN + SEG_MOST].astype(BF16)
        return carry

    def summed(w, offset):
        total = jnp.zeros((PROMPT_LEN, HEAD_DIM), F32)
        for s in range(SEGS):
            total = total + jnp.where(offsets[s] == offset, term[w, s], 0.0)
        return total

    def to_sibling(w):
        copies = []
        for i, away in enumerate((-1, 0, 1)):
            sib_send[w, i] = summed(w, 2 * away + 1 - 2 * core).astype(BF16)
        sib_send[w, 3] = summed(w, 6 * core - 3).astype(BF16)
        for i in (3, 0, 2, 1):
            copies.append(send(sib_send.at[w, i], sib_recv.at[w, i], sibling))
        return copies

    def to_far(w, copies):
        for copy in copies:
            copy.wait_recv()
        extra = sib_recv[w, 3].astype(F32)
        far_send[w, 0] = (summed(w, 4) + jnp.where(core == 0, extra, 0.0)).astype(BF16)
        far_send[w, 1] = (summed(w, -4) + jnp.where(core == 1, extra, 0.0)).astype(BF16)
        return [
            send(far_send.at[w, 0], far_recv.at[w, 0], right),
            send(far_send.at[w, 1], far_recv.at[w, 1], left),
        ]

    def to_near(w, copies):
        sent = []
        for i, device in enumerate((right, left)):
            copies[i].wait_recv()
            part = summed(w, 2 - 4 * i) + sib_recv[w, 2 - 2 * i].astype(F32) + far_recv[w, i].astype(F32)
            near_send[w, i] = part.astype(BF16)
            sent.append(send(near_send.at[w, i], near_recv.at[w, i], device))
        return sent

    def finish(w, copies):
        total = summed(w, 0) + sib_recv[w, 1].astype(F32)
        for i in range(2):
            copies[i].wait_recv()
            total = total + near_recv[w, i].astype(F32)
        dcache_out[:, w * HEAD_DIM : (w + 1) * HEAD_DIM] = total.astype(BF16)

    def give_back(window, staged, out, width, sem):
        parts = [window[:, g].reshape(SEGS * SEG_MOST, HEAD_DIM) for g in range(width // HEAD_DIM)]
        tokens = dot(unpick, jnp.concatenate(parts, axis=1), ((1,), (0,)))
        staged[...] = tokens.astype(BF16).reshape(N_HEAD, ROWS, width)
        copies = [send(staged.at[p], out.at[:, columns(head, width)], (dp, p)) for p in peers]
        own = pltpu.make_async_copy(staged.at[head], out.at[:, columns(head, width)], local_sem.at[sem])
        own.start()
        return copies, own

    arrived(0)
    lax.fori_loop(0, SEGS, weigh, 0)
    value_sib = to_sibling(1)
    arrived(1)
    value_far = to_far(1, value_sib)
    lax.fori_loop(0, SEGS, attend, 0)
    att_copies, att_own = give_back(win_o, att_send, att_out, OUT, 0)
    lax.fori_loop(0, SEGS, differentiate, 0)
    grad_copies, grad_own = give_back(win_g, dproj_send, dproj_out, PACK, 1)
    key_sib = to_sibling(0)
    value_near = to_near(1, value_far)
    key_far = to_far(0, key_sib)
    finish(1, value_near)
    key_near = to_near(0, key_far)
    finish(0, key_near)
    for copy in att_copies + grad_copies:
        copy.wait_recv()
    att_own.wait()
    grad_own.wait()
    sent = near[0] + near[1] + far[0] + far[1] + sib[0] + sib[1] + a2a[0] + a2a[1]
    sent += value_sib + value_far + value_near + key_sib + key_far + key_near + att_copies + grad_copies
    assert len(sent) == used[0] <= COPIES
    for copy in sent:
        copy.wait_send()


def local(projected, grad_output, prompt_cache, segment_ids, segment_prompt):
    hbm = pl.BlockSpec(memory_space=pl.ANY)
    vmem = pl.BlockSpec(memory_space=pltpu.VMEM)
    smem = pl.BlockSpec(memory_space=pltpu.SMEM)
    block = (PROMPT_LEN, HEAD_DIM)
    return pl.pallas_call(
        kernel,
        out_shape=(
            jax.ShapeDtypeStruct(grad_output.shape, BF16),
            jax.ShapeDtypeStruct(projected.shape, BF16),
            jax.ShapeDtypeStruct(prompt_cache.shape, BF16),
        ),
        in_specs=[vmem, smem, hbm, hbm, hbm],
        out_specs=(hbm, hbm, vmem),
        scratch_shapes=[
            pltpu.VMEM((N_HEAD, ROWS, PACK), BF16),
            pltpu.VMEM((N_HEAD, ROWS, OUT), BF16),
            pltpu.VMEM((9,) + block, BF16),
            pltpu.VMEM((9,) + block, BF16),
            pltpu.VMEM((SEGS, GROUP, SEG_MOST, HEAD_DIM), BF16),
            pltpu.VMEM((2, SEGS, HEAD_DIM, HEAD_DIM), BF16),
            pltpu.VMEM((SEGS, GROUP, SEG_MOST, HEAD_DIM), BF16),
            pltpu.VMEM((SEGS, STACK, KEYS), F32),
            pltpu.VMEM((2, SEGS) + block, F32),
            pltpu.VMEM((SEGS, GROUP, SEG_MOST, HEAD_DIM), BF16),
            pltpu.VMEM((SEGS, GROUP + 2, SEG_MOST, HEAD_DIM), BF16),
            pltpu.VMEM((N_HEAD, ROWS, OUT), BF16),
            pltpu.VMEM((N_HEAD, ROWS, PACK), BF16),
            pltpu.VMEM((2, 4) + block, BF16),
            pltpu.VMEM((2, 4) + block, BF16),
            pltpu.VMEM((2, 2) + block, BF16),
            pltpu.VMEM((2, 2) + block, BF16),
            pltpu.VMEM((2, 2) + block, BF16),
            pltpu.VMEM((2, 2) + block, BF16),
            pltpu.SemaphoreType.DMA((4,)),
            pltpu.SemaphoreType.DMA((COPIES,)),
            pltpu.SemaphoreType.DMA((COPIES,)),
        ],
        compiler_params=pltpu.CompilerParams(
            collective_id=0, has_side_effects=True, vmem_limit_bytes=62 << 20
        ),
    )(segment_ids, segment_prompt, projected, grad_output, prompt_cache)


def solution(mesh):
    return jax.shard_map(
        local,
        mesh=mesh,
        in_specs=(
            P(("dp", "head"), None),
            P(("dp", "head"), None),
            P("dp", "head"),
            P("dp", None),
            P("dp", None),
        ),
        out_specs=(P(("dp", "head"), None), P(("dp", "head"), None), P("dp", "head")),
        check_vma=False,
    )
```

time: 233 us -> 59.8 us (0.26)
  starting transfers between devices: 85.1 us -> 0 us
  Pallas kernels: 0 us -> 55.4 us
  local copies, waits for them, and re-layouts: 57.9 us -> 3.37 us
  waiting for transfers between devices: 38.7 us -> 0 us
  matrix products: 27 us -> 0 us
  other arithmetic: 18.7 us -> 0 us
  between operations: 3.97 us -> 0.65 us
    ppermute x16 -> x0, starting transfers between devices: 61 us -> none  [passed_along(): return lax.ppermute(block, axis, route)]
    pallas_call x0 -> x1, Pallas kernels: none -> 55.4 us  [local(): pl.pallas_call(kernel, out_shape=(jax.ShapeDtypeStruct(grad_output.shape,...]
    ppermute x16 -> x0, waiting for transfers between devices: 27.1 us -> none  [passed_along(): return lax.ppermute(block, axis, route)]
    dot_general x30 -> x0, matrix products: 27 us -> none  [product(): return jnp.einsum(form, left, right, preferred_element_type=jnp.float32)]
    all_to_all x4 -> x0, starting transfers between devices: 24.1 us -> none  [the longest x1 6.82 us: local(): lax.all_to_all(projected, 'head', split_axis=1, concat_axis=0, tiled=True)]
    slice x11 -> x0, local copies, waits for them, and re-layouts: 17.2 us -> none  [the longest x8 12.2 us: local(): slot_terms[distance + REACH]]
    all_to_all x4 -> x0, waiting for transfers between devices: 11.6 us -> none  [the longest x1 7.99 us: local(): lax.all_to_all(d_packed.reshape(row_count, -1), 'head', split_axis=0, con...]
    add x12 -> x0, local copies, waits for them, and re-layouts: 10.1 us -> none  [the longest x4 7.02 us: attend(): attended + place(product('kgtl,lkh->tkgh', rounded, prompt_values[segment...]
  transfers between devices with their start and end apart: 20 -> 0, of which waited for: 8 -> 0; matrix products, arithmetic and copies ran while one was open for 25% -> 0% of each run, Pallas kernels for 0% -> 0%
where the time goes in v1:
time: 59.8 us; the launch traced here: 59.4 us
  Pallas kernels  55.4 us (93%)
  local copies, waits for them, and re-layouts  3.37 us (6%)
  between operations  0.65 us (1%)
    pallas_call x1, Pallas kernels, local(): pl.pallas_call(kernel, out_shape=(jax.ShapeDtypeStruct(grad_output.shape,...  55.4 us
    unnamed x7, local copies, waits for them, and re-layouts  3.37 us

profile of v1, /device:TPU:1, one launch (start us, length us, event | category | flops | bytes accessed | tf_op | source)
XLA Modules:
  0.0 59.4 jit_solution(10501855044546231962)
XLA Ops:
  0.6 55.4 %shard_map.76 = (bf16[16,5120]{1,0:T(8,128)(2,1)}, bf16[16,7168]{1,0:T(8,128)(2,1)}, bf16[512,256]{1,0:T(8,128)(2,1)}) custom-call(s32[1,128]{1,0:T(1,128)} %ids_ref.1, s32[1,4]{1,0:T(1,128)} %owner_ref.1, bf16[16,7168]{1,0:T(8,128)(2,1)} %proj.1, bf16[16,5120]{1,0:T(8,128)(2,1)} %gout.1, bf16[512,256]{1,0:T(8,128)(2,1)} %cache.1), custom_call_target="tpu_custom_call" | custom-call | tf_op jit(solution)/shard_map/pallas_call | solution.py:285
  56.0 0.0 copy-start.1
  56.0 1.6 %copy.11 = bf16[16,5120]{1,0:T(8,128)(2,1)} copy(bf16[16,5120]{1,0:T(8,128)(2,1)} %get-tuple-element.6) | data formatting | bytes 327680
  57.7 0.0 copy-done.1
  57.7 0.0 copy-start
  57.7 0.7 %copy.12 = bf16[16,7168]{1,0:T(8,128)(2,1)} copy(bf16[16,7168]{1,0:T(8,128)(2,1)S(1)} %copy-done.1) | data formatting | bytes 458752
  58.4 0.3 copy-done
  58.7 0.7 %copy.13 = bf16[512,256]{1,0:T(8,128)(2,1)} copy(bf16[512,256]{1,0:T(8,128)(2,1)S(1)} %copy-done) | data formatting | bytes 524288
Async XLA Ops:
  56.0 1.6 %copy-start.1 = (bf16[16,7168]{1,0:T(8,128)(2,1)S(1)}, bf16[16,7168]{1,0:T(8,128)(2,1)}, u32[]{:S(2)}) copy-start(bf16[16,7168]{1,0:T(8,128)(2,1)} %get-tuple-element.7) | copy-start | bytes 688132
  57.7 1.0 %copy-start = (bf16[512,256]{1,0:T(8,128)(2,1)S(1)}, bf16[512,256]{1,0:T(8,128)(2,1)}, u32[]{:S(2)}) copy-start(bf16[512,256]{1,0:T(8,128)(2,1)} %get-tuple-element.8) | copy-start | bytes 786436

commit v2 on v1

v2 whole, which is shorter than its diff:
```python
import jax
import jax.numpy as jnp
from jax import lax
from jax.experimental import pallas as pl
from jax.experimental.pallas import tpu as pltpu
from jax.sharding import PartitionSpec as P

HEADS = 40
KV_HEADS = 8
HEAD_DIM = 128
GROUP = HEADS // KV_HEADS
TOK_DEV = 128
PROMPT_LEN = 512
SEGS = 4
REACH = 4
SEG_MOST = 64
N_DP = 64
CHIPS = N_DP // 2
N_HEAD = 8
ROWS = TOK_DEV // N_HEAD
PACK = (GROUP + 2) * HEAD_DIM
OUT = GROUP * HEAD_DIM
STACK = GROUP * SEG_MOST
KEYS = PROMPT_LEN + HEAD_DIM
SCALE = HEAD_DIM**-0.5
LOG2E = 1.4426950408889634
MESH = pl.DeviceIdType.MESH
F32 = jnp.float32
BF16 = jnp.bfloat16
COPIES = 80
HALF = PROMPT_LEN // 2


def dot(left, right, contract):
    return lax.dot_general(left, right, (contract, ((), ())), preferred_element_type=F32)


def kernel(
    ids_ref, owner_ref, proj, gout, cache,
    att_out, dproj_out, dcache_out,
    pk, dk, keys, values, win_q, win_kv, win_d, prob, prob_b, dscore_b, term, win_o, win_g, att_send, dproj_send,
    sib_send, sib_recv, far_send, far_recv, near_send, near_recv,
    local_sem, send_sem, recv_sem,
):
    dp = lax.axis_index("dp")
    head = lax.axis_index("head")
    chip = dp // 2
    core = lax.rem(dp, 2)
    sibling = (dp + 1 - 2 * core, head)
    right = (lax.rem(chip + 1, CHIPS) * 2 + core, head)
    left = (lax.rem(chip + CHIPS - 1, CHIPS) * 2 + core, head)
    peers = [lax.rem(head + j, N_HEAD) for j in range(1, N_HEAD)]
    kv = (keys, values)
    sent = []

    def send(src, dst, device):
        i = len(sent)
        copy = pltpu.make_async_remote_copy(
            src_ref=src, dst_ref=dst, send_sem=send_sem.at[i], recv_sem=recv_sem.at[i],
            device_id=device, device_id_type=MESH,
        )
        copy.start()
        sent.append(copy)
        return copy

    def columns(index, width):
        return pl.ds(pl.multiple_of(index * width, HEAD_DIM), width)

    def feature(w):
        return pl.ds(w * HEAD_DIM, HEAD_DIM)

    halves = [pl.ds(i * HALF, HALF) for i in range(2)]

    own_kv = [pltpu.make_async_copy(cache.at[:, feature(w)], kv[w].at[2], local_sem.at[w]) for w in range(2)]
    own_proj = pltpu.make_async_copy(proj.at[:, columns(head, PACK)], pk.at[head], local_sem.at[2])
    own_gout = pltpu.make_async_copy(gout.at[:, columns(head, OUT)], dk.at[head], local_sem.at[3])
    for copy in own_kv + [own_proj, own_gout]:
        copy.start()
    barrier = pltpu.get_barrier_semaphore()
    partners = [right, left, sibling] + [(dp, p) for p in peers]
    for partner in partners:
        pl.semaphore_signal(barrier, inc=1, device_id=partner, device_id_type=MESH)

    ids = ids_ref[...]
    position = lax.broadcasted_iota(jnp.int32, (1, TOK_DEV), 1)
    first = jnp.zeros((1, TOK_DEV), jnp.int32)
    for s in range(SEGS):
        before = jnp.sum((ids < s).astype(jnp.int32), axis=1, keepdims=True)
        first = first + jnp.where(ids == s, before, 0)
    row = (ids * SEG_MOST + position - first).astype(F32)
    rows = lax.broadcasted_iota(jnp.int32, (SEGS * SEG_MOST, TOK_DEV), 0).astype(F32)
    pick = (jnp.broadcast_to(row, rows.shape) == rows).astype(BF16)
    row_t = jnp.transpose(jnp.broadcast_to(row, (TOK_DEV, TOK_DEV)))
    cols = lax.broadcasted_iota(jnp.int32, (TOK_DEV, SEGS * SEG_MOST), 1).astype(F32)
    unpick = (jnp.concatenate([row_t, row_t], axis=1) == cols).astype(BF16)

    offsets, slots = [], []
    for s in range(SEGS):
        offset = lax.rem(owner_ref[0, s] - dp + N_DP + REACH, N_DP) - REACH
        odd = lax.rem(offset + 8, 2)
        away = jnp.where(odd == 1, offset - 1 + 2 * core, offset) // 2
        slot = jnp.where(
            odd == 0, jnp.clip(away, -2, 2) + 2,
            jnp.where(away == 0, 5, jnp.where(away == 1, 6, jnp.where(away == -1, 7, 8))),
        )
        offsets.append(offset)
        slots.append(slot)

    pl.semaphore_wait(barrier, len(partners))

    def start_near(w):
        copies = []
        for half in halves:
            block = cache.at[half, feature(w)]
            copies.append(send(block, kv[w].at[1, half], right))
            copies.append(send(block, kv[w].at[3, half], left))
        return copies

    def relay(w, i, near):
        near[2 * i].wait_recv()
        from_left = send(kv[w].at[1, halves[i]], kv[w].at[0, halves[i]], right)
        near[2 * i + 1].wait_recv()
        from_right = send(kv[w].at[3, halves[i]], kv[w].at[4, halves[i]], left)
        return [from_left, from_right]

    def share_near(w):
        return [send(kv[w].at[1], kv[w].at[7], sibling), send(kv[w].at[3], kv[w].at[6], sibling)]

    def share_far(w, far):
        for copy in far:
            copy.wait_recv()
        return [send(kv[w].at[4 - 4 * core], kv[w].at[8], sibling)]

    near_k = start_near(0)
    sib_k = [send(cache.at[:, feature(0)], keys.at[5], sibling)]
    a2a_p = [send(proj.at[:, columns(p, PACK)], pk.at[head], (dp, p)) for p in peers]
    far_k = relay(0, 0, near_k)
    far_k += relay(0, 1, near_k)
    near_v = start_near(1)
    sib_k += share_near(0)
    a2a_g = [send(gout.at[:, columns(p, OUT)], dk.at[head], (dp, p)) for p in peers]
    sib_v = [send(cache.at[:, feature(1)], values.at[5], sibling)]

    def spread(picked, window):
        for g in range(GROUP):
            part = picked[:, g * HEAD_DIM : (g + 1) * HEAD_DIM]
            window[:, g] = part.reshape(SEGS, SEG_MOST, HEAD_DIM)

    def gather_proj():
        own_proj.wait()
        for copy in a2a_p:
            copy.wait_recv()
        picked = dot(pick, pk[...].reshape(TOK_DEV, PACK), ((1,), (0,))).astype(BF16)
        spread(picked, win_q)
        for w in range(2):
            own = picked[:, OUT + w * HEAD_DIM : OUT + (w + 1) * HEAD_DIM].reshape(SEGS, SEG_MOST, HEAD_DIM)
            win_kv[w] = jnp.concatenate([own, jnp.zeros_like(own)], axis=1)

    def gather_gout():
        own_gout.wait()
        for copy in a2a_g:
            copy.wait_recv()
        spread(dot(pick, dk[...].reshape(TOK_DEV, OUT), ((1,), (0,))).astype(BF16), win_d)

    def all_rows(w, s):
        return jnp.concatenate([kv[w][slots[s]], win_kv[w, s]], axis=0)

    def queries(s):
        return win_q[s].reshape(STACK, HEAD_DIM)

    def dout(s):
        return win_d[s].reshape(STACK, HEAD_DIM)

    key_at = lax.broadcasted_iota(jnp.int32, (STACK, HEAD_DIM), 1)
    row_at = lax.rem(lax.broadcasted_iota(jnp.int32, (STACK, HEAD_DIM), 0), SEG_MOST)

    def weigh(s):
        scores = dot(queries(s), all_rows(0, s), ((1,), (1,)))
        own = jnp.where(key_at <= row_at, scores[:, PROMPT_LEN:], -1e30)
        scores = jnp.concatenate([scores[:, :PROMPT_LEN], own], axis=1)
        top = jnp.max(scores, axis=1, keepdims=True)
        expo = jnp.exp2((scores - top) * (SCALE * LOG2E))
        weights = expo * (1.0 / jnp.sum(expo, axis=1, keepdims=True))
        prob[s] = weights
        prob_b[s] = weights.astype(BF16)

    def value_terms(s):
        dvalue = dot(prob_b[s], dout(s), ((0,), (0,)))
        term[1, s] = dvalue[:PROMPT_LEN]
        win_g[s, GROUP + 1] = dvalue[PROMPT_LEN : PROMPT_LEN + SEG_MOST].astype(BF16)

    def attend(s):
        out = dot(prob_b[s], all_rows(1, s), ((1,), (0,))).astype(BF16)
        win_o[s] = out.reshape(GROUP, SEG_MOST, HEAD_DIM)

    def key_terms(s):
        out = win_o[s].reshape(STACK, HEAD_DIM)
        delta = jnp.sum(dout(s).astype(F32) * out.astype(F32), axis=1, keepdims=True)
        dweight = dot(dout(s), all_rows(1, s), ((1,), (1,)))
        dscore = (prob[s] * (dweight - delta) * SCALE).astype(BF16)
        dscore_b[s] = dscore
        dkey = dot(dscore, queries(s), ((0,), (0,)))
        term[0, s] = dkey[:PROMPT_LEN]
        win_g[s, GROUP] = dkey[PROMPT_LEN : PROMPT_LEN + SEG_MOST].astype(BF16)

    def query_terms(s):
        dquery = dot(dscore_b[s], all_rows(0, s), ((1,), (0,))).astype(BF16)
        win_g[s, :GROUP] = dquery.reshape(GROUP, SEG_MOST, HEAD_DIM)

    def summed(w, offset, part):
        total = jnp.zeros((part.size, HEAD_DIM), F32)
        for s in range(SEGS):
            total = total + jnp.where(offsets[s] == offset, term[w, s, part], 0.0)
        return total

    whole = pl.ds(0, PROMPT_LEN)

    def to_sibling(w):
        copies = [None] * 4
        for i, offset in ((3, 6 * core - 3), (0, -1 - 2 * core), (2, 3 - 2 * core), (1, 1 - 2 * core)):
            sib_send[w, i] = summed(w, offset, whole).astype(BF16)
            copies[i] = send(sib_send.at[w, i], sib_recv.at[w, i], sibling)
        return copies

    def to_far(w, sib):
        sib[3].wait_recv()
        copies = []
        for half in halves:
            extra = sib_recv[w, 3, half].astype(F32)
            far_send[w, 0, half] = (summed(w, 4, half) + jnp.where(core == 0, extra, 0.0)).astype(BF16)
            copies.append(send(far_send.at[w, 0, half], far_recv.at[w, 0, half], right))
            far_send[w, 1, half] = (summed(w, -4, half) + jnp.where(core == 1, extra, 0.0)).astype(BF16)
            copies.append(send(far_send.at[w, 1, half], far_recv.at[w, 1, half], left))
        return copies

    def to_near(w, h, sib, far):
        half = halves[h]
        copies = []
        for i, device in enumerate((right, left)):
            if h == 0:
                sib[2 - 2 * i].wait_recv()
            part = summed(w, 2 - 4 * i, half) + sib_recv[w, 2 - 2 * i, half].astype(F32)
            far[2 * h + i].wait_recv()
            near_send[w, i, half] = (part + far_recv[w, i, half].astype(F32)).astype(BF16)
            copies.append(send(near_send.at[w, i, half], near_recv.at[w, i, half], device))
        return copies

    def finish(w, h, sib, near):
        half = halves[h]
        if h == 0:
            sib[1].wait_recv()
        total = summed(w, 0, half) + sib_recv[w, 1, half].astype(F32)
        for i in range(2):
            near[2 * h + i].wait_recv()
            total = total + near_recv[w, i, half].astype(F32)
        dcache_out[half, feature(w)] = total.astype(BF16)

    def give_back(window, staged, out, width, sem):
        parts = [window[:, g].reshape(SEGS * SEG_MOST, HEAD_DIM) for g in range(width // HEAD_DIM)]
        tokens = dot(unpick, jnp.concatenate(parts, axis=1), ((1,), (0,)))
        staged[...] = tokens.astype(BF16).reshape(N_HEAD, ROWS, width)
        copies = [send(staged.at[p], out.at[:, columns(head, width)], (dp, p)) for p in peers]
        own = pltpu.make_async_copy(staged.at[head], out.at[:, columns(head, width)], local_sem.at[sem])
        own.start()
        return copies, own

    gather_proj()
    sib_k += share_far(0, far_k)
    own_kv[0].wait()
    for copy in sib_k:
        copy.wait_recv()
    weigh(0)
    far_v = relay(1, 0, near_v)
    weigh(1)
    far_v += relay(1, 1, near_v)
    sib_v += share_near(1)
    weigh(2)
    weigh(3)
    gather_gout()
    for s in range(SEGS):
        value_terms(s)
    value_sib = to_sibling(1)
    sib_v += share_far(1, far_v)
    value_far = to_far(1, value_sib)
    own_kv[1].wait()
    for copy in sib_v:
        copy.wait_recv()
    for s in range(SEGS):
        attend(s)
    att_copies, att_own = give_back(win_o, att_send, att_out, OUT, 0)
    key_terms(0)
    key_terms(1)
    value_near = to_near(1, 0, value_sib, value_far)
    key_terms(2)
    key_terms(3)
    key_sib = to_sibling(0)
    value_near += to_near(1, 1, value_sib, value_far)
    for s in range(SEGS):
        query_terms(s)
    key_far = to_far(0, key_sib)
    grad_copies, grad_own = give_back(win_g, dproj_send, dproj_out, PACK, 1)
    finish(1, 0, value_sib, value_near)
    finish(1, 1, value_sib, value_near)
    key_near = to_near(0, 0, key_sib, key_far)
    key_near += to_near(0, 1, key_sib, key_far)
    finish(0, 0, key_sib, key_near)
    finish(0, 1, key_sib, key_near)
    for copy in att_copies + grad_copies:
        copy.wait_recv()
    att_own.wait()
    grad_own.wait()
    assert len(sent) <= COPIES
    for copy in sent:
        copy.wait_send()


def hand_over(att, dproj, dcache, att_out, dproj_out, dcache_out, sems):
    copies = [
        pltpu.make_async_copy(src, dst, sems.at[i])
        for i, (src, dst) in enumerate(((att, att_out), (dproj, dproj_out), (dcache, dcache_out)))
    ]
    for copy in copies:
        copy.start()
    for copy in copies:
        copy.wait()


def local(projected, grad_output, prompt_cache, segment_ids, segment_prompt):
    hbm = pl.BlockSpec(memory_space=pltpu.HBM)
    vmem = pl.BlockSpec(memory_space=pltpu.VMEM)
    smem = pl.BlockSpec(memory_space=pltpu.SMEM)
    block = (PROMPT_LEN, HEAD_DIM)
    results = (
        jax.ShapeDtypeStruct(grad_output.shape, BF16),
        jax.ShapeDtypeStruct(projected.shape, BF16),
        jax.ShapeDtypeStruct(prompt_cache.shape, BF16),
    )
    outs = pl.pallas_call(
        kernel,
        out_shape=tuple(pltpu.VMEM(r.shape, BF16) for r in results),
        in_specs=[vmem, smem, hbm, hbm, hbm],
        out_specs=(vmem, vmem, vmem),
        scratch_shapes=[
            pltpu.VMEM((N_HEAD, ROWS, PACK), BF16),
            pltpu.VMEM((N_HEAD, ROWS, OUT), BF16),
            pltpu.VMEM((9,) + block, BF16),
            pltpu.VMEM((9,) + block, BF16),
            pltpu.VMEM((SEGS, GROUP, SEG_MOST, HEAD_DIM), BF16),
            pltpu.VMEM((2, SEGS, HEAD_DIM, HEAD_DIM), BF16),
            pltpu.VMEM((SEGS, GROUP, SEG_MOST, HEAD_DIM), BF16),
            pltpu.VMEM((SEGS, STACK, KEYS), F32),
            pltpu.VMEM((SEGS, STACK, KEYS), BF16),
            pltpu.VMEM((SEGS, STACK, KEYS), BF16),
            pltpu.VMEM((2, SEGS) + block, F32),
            pltpu.VMEM((SEGS, GROUP, SEG_MOST, HEAD_DIM), BF16),
            pltpu.VMEM((SEGS, GROUP + 2, SEG_MOST, HEAD_DIM), BF16),
            pltpu.VMEM((N_HEAD, ROWS, OUT), BF16),
            pltpu.VMEM((N_HEAD, ROWS, PACK), BF16),
            pltpu.VMEM((2, 4) + block, BF16),
            pltpu.VMEM((2, 4) + block, BF16),
            pltpu.VMEM((2, 2) + block, BF16),
            pltpu.VMEM((2, 2) + block, BF16),
            pltpu.VMEM((2, 2) + block, BF16),
            pltpu.VMEM((2, 2) + block, BF16),
            pltpu.SemaphoreType.DMA((4,)),
            pltpu.SemaphoreType.DMA((COPIES,)),
            pltpu.SemaphoreType.DMA((COPIES,)),
        ],
        compiler_params=pltpu.CompilerParams(
            collective_id=0, has_side_effects=True, vmem_limit_bytes=60 << 20
        ),
    )(segment_ids, segment_prompt, projected, grad_output, prompt_cache)
    return pl.pallas_call(
        hand_over,
        out_shape=results,
        in_specs=[vmem] * 3,
        out_specs=(hbm,) * 3,
        scratch_shapes=[pltpu.SemaphoreType.DMA((3,))],
        compiler_params=pltpu.CompilerParams(vmem_limit_bytes=8 << 20),
    )(*outs)


def solution(mesh):
    return jax.shard_map(
        local,
        mesh=mesh,
        in_specs=(
            P(("dp", "head"), None),
            P(("dp", "head"), None),
            P("dp", "head"),
            P("dp", None),
            P("dp", None),
        ),
        out_specs=(P(("dp", "head"), None), P(("dp", "head"), None), P("dp", "head")),
        check_vma=False,
    )
```

time: 59.8 us -> 56 us (0.936)
  local copies, waits for them, and re-layouts: 3.37 us -> 0 us
    unnamed x7 -> x0, local copies, waits for them, and re-layouts: 3.37 us -> none
    pallas_call x1 -> x2, Pallas kernels: 55.4 us -> 55.3 us  [the longest x1 54.4 us: local(): pl.pallas_call(kernel, out_shape=tuple((pltpu.VMEM(r.shape, BF16) for r i...]
where the time goes in v2:
time: 56 us; the launch traced here: 55.9 us
  Pallas kernels  55.3 us (99%)
  between operations  0.64 us (1%)
    pallas_call x1, Pallas kernels, local(): pl.pallas_call(kernel, out_shape=tuple((pltpu.VMEM(r.shape, BF16) for r i...  54.4 us

profile of v2, /device:TPU:1, one launch (start us, length us, event | category | flops | bytes accessed | tf_op | source)
XLA Modules:
  0.0 55.9 jit_solution(8966670548169124823)
XLA Ops:
  0.6 54.4 %shard_map.76 = (bf16[16,5120]{1,0:T(8,128)(2,1)S(1)}, bf16[16,7168]{1,0:T(8,128)(2,1)S(1)}, bf16[512,256]{1,0:T(8,128)(2,1)S(1)}) custom-call(s32[1,128]{1,0:T(1,128)} %ids_ref.1, s32[1,4]{1,0:T(1,128)} %owner_ref.1, bf16[16,7168]{1,0:T(8,128)(2,1)} %proj.1, bf16[16,5120]{1,0:T(8,128)(2,1)} %gout.1, bf16[512,256]{1,0:T(8,128)(2,1)} %cache.1), custom_call_target="tpu_custom_call" | custom-call | tf_op jit(solution)/shard_map/pallas_call | solution.py:338
  55.0 0.9 %shard_map.77 = (bf16[16,5120]{1,0:T(8,128)(2,1)}, bf16[16,7168]{1,0:T(8,128)(2,1)}, bf16[512,256]{1,0:T(8,128)(2,1)}) custom-call(bf16[16,5120]{1,0:T(8,128)(2,1)S(1)} %get-tuple-element.6.att, bf16[16,7168]{1,0:T(8,128)(2,1)S(1)} %get-tuple-element.7.dproj, bf16[512,256]{1,0:T(8,128)(2,1)S(1)} %get-tuple-element.8.dcache), custom_call_target="tpu_custom_call" | custom-call | tf_op jit(solution)/shard_map/pallas_call | solution.py:373

commit v3 on v2

--- a/solution.py
+++ b/solution.py
@@ -36,9 +36,9 @@
 
 
 def kernel(
-    ids_ref, owner_ref, proj, gout, cache,
+    ids_hbm, owner_hbm, proj, gout, cache,
     att_out, dproj_out, dcache_out,
-    pk, dk, keys, values, win_q, win_kv, win_d, prob, prob_b, dscore_b, term, win_o, win_g, att_send, dproj_send,
+    ids_ref, owner_ref, pk, dk, keys, values, win_q, win_kv, win_d, prob, prob_b, dscore_b, term, win_o, win_g, att_send, dproj_send,
     sib_send, sib_recv, far_send, far_recv, near_send, near_recv,
     local_sem, send_sem, recv_sem,
 ):
@@ -49,7 +49,7 @@
     sibling = (dp + 1 - 2 * core, head)
     right = (lax.rem(chip + 1, CHIPS) * 2 + core, head)
     left = (lax.rem(chip + CHIPS - 1, CHIPS) * 2 + core, head)
-    peers = [lax.rem(head + j, N_HEAD) for j in range(1, N_HEAD)]
+    peers = [lax.rem(head + j, N_HEAD) for j in (4, 3, 5, 2, 6, 1, 7)]
     kv = (keys, values)
     sent = []
 
@@ -71,15 +71,21 @@
 
     halves = [pl.ds(i * HALF, HALF) for i in range(2)]
 
+    barrier = pltpu.get_barrier_semaphore()
+    partners = [right, left] + [(dp, p) for p in peers] + [sibling]
+    for partner in partners:
+        pl.semaphore_signal(barrier, inc=1, device_id=partner, device_id_type=MESH)
+    small = [
+        pltpu.make_async_copy(ids_hbm, ids_ref, local_sem.at[4]),
+        pltpu.make_async_copy(owner_hbm, owner_ref, local_sem.at[5]),
+    ]
     own_kv = [pltpu.make_async_copy(cache.at[:, feature(w)], kv[w].at[2], local_sem.at[w]) for w in range(2)]
     own_proj = pltpu.make_async_copy(proj.at[:, columns(head, PACK)], pk.at[head], local_sem.at[2])
     own_gout = pltpu.make_async_copy(gout.at[:, columns(head, OUT)], dk.at[head], local_sem.at[3])
-    for copy in own_kv + [own_proj, own_gout]:
+    for copy in small + own_kv + [own_proj, own_gout]:
         copy.start()
-    barrier = pltpu.get_barrier_semaphore()
-    partners = [right, left, sibling] + [(dp, p) for p in peers]
-    for partner in partners:
-        pl.semaphore_signal(barrier, inc=1, device_id=partner, device_id_type=MESH)
+    for copy in small:
+        copy.wait()
 
     ids = ids_ref[...]
     position = lax.broadcasted_iota(jnp.int32, (1, TOK_DEV), 1)
@@ -269,8 +275,8 @@
     own_kv[0].wait()
     for copy in sib_k:
         copy.wait_recv()
+    far_v = relay(1, 0, near_v)
     weigh(0)
-    far_v = relay(1, 0, near_v)
     weigh(1)
     far_v += relay(1, 1, near_v)
     sib_v += share_near(1)
@@ -288,21 +294,19 @@
     for s in range(SEGS):
         attend(s)
     att_copies, att_own = give_back(win_o, att_send, att_out, OUT, 0)
-    key_terms(0)
-    key_terms(1)
+    for s in range(SEGS):
+        key_terms(s)
+    key_sib = to_sibling(0)
+    for s in range(SEGS):
+        query_terms(s)
+    grad_copies, grad_own = give_back(win_g, dproj_send, dproj_out, PACK, 1)
+    key_far = to_far(0, key_sib)
     value_near = to_near(1, 0, value_sib, value_far)
-    key_terms(2)
-    key_terms(3)
-    key_sib = to_sibling(0)
     value_near += to_near(1, 1, value_sib, value_far)
-    for s in range(SEGS):
-        query_terms(s)
-    key_far = to_far(0, key_sib)
-    grad_copies, grad_own = give_back(win_g, dproj_send, dproj_out, PACK, 1)
+    key_near = to_near(0, 0, key_sib, key_far)
+    key_near += to_near(0, 1, key_sib, key_far)
     finish(1, 0, value_sib, value_near)
     finish(1, 1, value_sib, value_near)
-    key_near = to_near(0, 0, key_sib, key_far)
-    key_near += to_near(0, 1, key_sib, key_far)
     finish(0, 0, key_sib, key_near)
     finish(0, 1, key_sib, key_near)
     for copy in att_copies + grad_copies:
@@ -328,7 +332,6 @@
 def local(projected, grad_output, prompt_cache, segment_ids, segment_prompt):
     hbm = pl.BlockSpec(memory_space=pltpu.HBM)
     vmem = pl.BlockSpec(memory_space=pltpu.VMEM)
-    smem = pl.BlockSpec(memory_space=pltpu.SMEM)
     block = (PROMPT_LEN, HEAD_DIM)
     results = (
         jax.ShapeDtypeStruct(grad_output.shape, BF16),
@@ -338,9 +341,11 @@
     outs = pl.pallas_call(
         kernel,
         out_shape=tuple(pltpu.VMEM(r.shape, BF16) for r in results),
-        in_specs=[vmem, smem, hbm, hbm, hbm],
+        in_specs=[hbm] * 5,
         out_specs=(vmem, vmem, vmem),
         scratch_shapes=[
+            pltpu.VMEM(segment_ids.shape, jnp.int32),
+            pltpu.SMEM(segment_prompt.shape, jnp.int32),
             pltpu.VMEM((N_HEAD, ROWS, PACK), BF16),
             pltpu.VMEM((N_HEAD, ROWS, OUT), BF16),
             pltpu.VMEM((9,) + block, BF16),
@@ -362,7 +367,7 @@
             pltpu.VMEM((2, 2) + block, BF16),
             pltpu.VMEM((2, 2) + block, BF16),
             pltpu.VMEM((2, 2) + block, BF16),
-            pltpu.SemaphoreType.DMA((4,)),
+            pltpu.SemaphoreType.DMA((6,)),
             pltpu.SemaphoreType.DMA((COPIES,)),
             pltpu.SemaphoreType.DMA((COPIES,)),
         ],

time: 56 us -> 54 us (0.964)
  Pallas kernels: 55.3 us -> 53.2 us
    pallas_call x1, Pallas kernels: 54.4 us -> 52.3 us  [local(): pl.pallas_call(kernel, out_shape=tuple((pltpu.VMEM(r.shape, BF16) for r i...]
where the time goes in v3:
time: 54 us; the launch traced here: 53.8 us
  Pallas kernels  53.2 us (99%)
  between operations  0.64 us (1%)
    pallas_call x1, Pallas kernels, local(): pl.pallas_call(kernel, out_shape=tuple((pltpu.VMEM(r.shape, BF16) for r i...  52.3 us

profile of v3, /device:TPU:1, one launch (start us, length us, event | category | flops | bytes accessed | tf_op | source)
XLA Modules:
  0.0 53.8 jit_solution(11348693403688944727)
XLA Ops:
  0.6 52.3 %shard_map.76 = (bf16[16,5120]{1,0:T(8,128)(2,1)S(1)}, bf16[16,7168]{1,0:T(8,128)(2,1)S(1)}, bf16[512,256]{1,0:T(8,128)(2,1)S(1)}) custom-call(s32[1,128]{1,0:T(1,128)} %ids_hbm.1, s32[1,4]{1,0:T(1,128)} %owner_hbm.1, bf16[16,7168]{1,0:T(8,128)(2,1)} %proj.1, bf16[16,5120]{1,0:T(8,128)(2,1)} %gout.1, bf16[512,256]{1,0:T(8,128)(2,1)} %cache.1), custom_call_target="tpu_custom_call" | custom-call | tf_op jit(solution)/shard_map/pallas_call | solution.py:341
  53.0 0.9 %shard_map.77 = (bf16[16,5120]{1,0:T(8,128)(2,1)}, bf16[16,7168]{1,0:T(8,128)(2,1)}, bf16[512,256]{1,0:T(8,128)(2,1)}) custom-call(bf16[16,5120]{1,0:T(8,128)(2,1)S(1)} %get-tuple-element.6.att, bf16[16,7168]{1,0:T(8,128)(2,1)S(1)} %get-tuple-element.7.dproj, bf16[512,256]{1,0:T(8,128)(2,1)S(1)} %get-tuple-element.8.dcache), custom_call_target="tpu_custom_call" | custom-call | tf_op jit(solution)/shard_map/pallas_call | solution.py:378

commit v4 on v3

--- a/solution.py
+++ b/solution.py
@@ -40,7 +40,7 @@
     att_out, dproj_out, dcache_out,
     ids_ref, owner_ref, pk, dk, keys, values, win_q, win_kv, win_d, prob, prob_b, dscore_b, term, win_o, win_g, att_send, dproj_send,
     sib_send, sib_recv, far_send, far_recv, near_send, near_recv,
-    local_sem, send_sem, recv_sem,
+    local_sem, send_sem, recv_sem, ring_sem,
 ):
     dp = lax.axis_index("dp")
     head = lax.axis_index("head")
@@ -49,7 +49,7 @@
     sibling = (dp + 1 - 2 * core, head)
     right = (lax.rem(chip + 1, CHIPS) * 2 + core, head)
     left = (lax.rem(chip + CHIPS - 1, CHIPS) * 2 + core, head)
-    peers = [lax.rem(head + j, N_HEAD) for j in (4, 3, 5, 2, 6, 1, 7)]
+    peers = [lax.rem(head + j, N_HEAD) for j in (1, 7, 2, 6, 3, 5, 4)]
     kv = (keys, values)
     sent = []
 
@@ -72,7 +72,7 @@
     halves = [pl.ds(i * HALF, HALF) for i in range(2)]
 
     barrier = pltpu.get_barrier_semaphore()
-    partners = [right, left] + [(dp, p) for p in peers] + [sibling]
+    partners = [right, left, (dp, peers[0]), (dp, peers[1]), sibling]
     for partner in partners:
         pl.semaphore_signal(barrier, inc=1, device_id=partner, device_id_type=MESH)
     small = [
@@ -138,14 +138,31 @@
         return [send(kv[w].at[4 - 4 * core], kv[w].at[8], sibling)]
 
     near_k = start_near(0)
+    near_v = start_near(1)
     sib_k = [send(cache.at[:, feature(0)], keys.at[5], sibling)]
-    a2a_p = [send(proj.at[:, columns(p, PACK)], pk.at[head], (dp, p)) for p in peers]
+    sib_v = [send(cache.at[:, feature(1)], values.at[5], sibling)]
+
+    def next_round():
+        for i in range(2):
+            pl.semaphore_signal(ring_sem.at[i], inc=1, device_id=(dp, peers[i]), device_id_type=MESH)
+        for i in range(2):
+            pl.semaphore_wait(ring_sem.at[i], 1)
+
+    def exchange(block, staged, width, chosen):
+        return [send(block.at[:, columns(p, width)], staged.at[head], (dp, p)) for p in chosen]
+
+    a2a_p = exchange(proj, pk, PACK, peers[:2])
+    a2a_g = []
+    for distance in range(1, 4):
+        next_round()
+        a2a_p += exchange(proj, pk, PACK, peers[2 * distance : 2 * distance + 2])
+    a2a_g += exchange(gout, dk, OUT, peers)
     far_k = relay(0, 0, near_k)
     far_k += relay(0, 1, near_k)
-    near_v = start_near(1)
     sib_k += share_near(0)
-    a2a_g = [send(gout.at[:, columns(p, OUT)], dk.at[head], (dp, p)) for p in peers]
-    sib_v = [send(cache.at[:, feature(1)], values.at[5], sibling)]
+    far_v = relay(1, 0, near_v)
+    far_v += relay(1, 1, near_v)
+    sib_v += share_near(1)
 
     def spread(picked, window):
         for g in range(GROUP):
@@ -275,13 +292,8 @@
     own_kv[0].wait()
     for copy in sib_k:
         copy.wait_recv()
-    far_v = relay(1, 0, near_v)
-    weigh(0)
-    weigh(1)
-    far_v += relay(1, 1, near_v)
-    sib_v += share_near(1)
-    weigh(2)
-    weigh(3)
+    for s in range(SEGS):
+        weigh(s)
     gather_gout()
     for s in range(SEGS):
         value_terms(s)
@@ -370,6 +382,7 @@
             pltpu.SemaphoreType.DMA((6,)),
             pltpu.SemaphoreType.DMA((COPIES,)),
             pltpu.SemaphoreType.DMA((COPIES,)),
+            pltpu.SemaphoreType.REGULAR((2,)),
         ],
         compiler_params=pltpu.CompilerParams(
             collective_id=0, has_side_effects=True, vmem_limit_bytes=60 << 20

time: 54 us -> 50.7 us (0.939)
  Pallas kernels: 53.2 us -> 49.9 us
    pallas_call x1, Pallas kernels: 52.3 us -> 49 us  [local(): pl.pallas_call(kernel, out_shape=tuple((pltpu.VMEM(r.shape, BF16) for r i...]
where the time goes in v4:
time: 50.7 us; the launch traced here: 50.6 us
  Pallas kernels  49.9 us (98%)
  between operations  0.64 us (1%)
    pallas_call x1, Pallas kernels, local(): pl.pallas_call(kernel, out_shape=tuple((pltpu.VMEM(r.shape, BF16) for r i...  49 us

profile of v4, /device:TPU:1, one launch (start us, length us, event | category | flops | bytes accessed | tf_op | source)
XLA Modules:
  0.0 50.6 jit_solution(17038965758754575089)
XLA Ops:
  0.6 49.0 %shard_map.76 = (bf16[16,5120]{1,0:T(8,128)(2,1)S(1)}, bf16[16,7168]{1,0:T(8,128)(2,1)S(1)}, bf16[512,256]{1,0:T(8,128)(2,1)S(1)}) custom-call(s32[1,128]{1,0:T(1,128)} %ids_hbm.1, s32[1,4]{1,0:T(1,128)} %owner_hbm.1, bf16[16,7168]{1,0:T(8,128)(2,1)} %proj.1, bf16[16,5120]{1,0:T(8,128)(2,1)} %gout.1, bf16[512,256]{1,0:T(8,128)(2,1)} %cache.1), custom_call_target="tpu_custom_call" | custom-call | tf_op jit(solution)/shard_map/pallas_call | solution.py:353
  49.7 0.9 %shard_map.77 = (bf16[16,5120]{1,0:T(8,128)(2,1)}, bf16[16,7168]{1,0:T(8,128)(2,1)}, bf16[512,256]{1,0:T(8,128)(2,1)}) custom-call(bf16[16,5120]{1,0:T(8,128)(2,1)S(1)} %get-tuple-element.6.att, bf16[16,7168]{1,0:T(8,128)(2,1)S(1)} %get-tuple-element.7.dproj, bf16[512,256]{1,0:T(8,128)(2,1)S(1)} %get-tuple-element.8.dcache), custom_call_target="tpu_custom_call" | custom-call | tf_op jit(solution)/shard_map/pallas_call | solution.py:391

commit v5 on v4

--- a/solution.py
+++ b/solution.py
@@ -16,6 +16,7 @@
 SEG_MOST = 64
 N_DP = 64
 CHIPS = N_DP // 2
+CHIPS_Z = 8
 N_HEAD = 8
 ROWS = TOK_DEV // N_HEAD
 PACK = (GROUP + 2) * HEAD_DIM
@@ -53,21 +54,29 @@
     kv = (keys, values)
     sent = []
 
-    def send(src, dst, device):
+    def prepare(src, dst, device):
         i = len(sent)
         copy = pltpu.make_async_remote_copy(
             src_ref=src, dst_ref=dst, send_sem=send_sem.at[i], recv_sem=recv_sem.at[i],
             device_id=device, device_id_type=MESH,
         )
-        copy.start()
         sent.append(copy)
         return copy
 
+    def send(src, dst, device):
+        copy = prepare(src, dst, device)
+        copy.start()
+        return copy
+
     def columns(index, width):
         return pl.ds(pl.multiple_of(index * width, HEAD_DIM), width)
 
     def feature(w):
         return pl.ds(w * HEAD_DIM, HEAD_DIM)
+
+    z = lax.rem(chip, CHIPS_Z)
+    slow = (z == 0, z == CHIPS_Z - 1)
+    fast = (z != 0, z != CHIPS_Z - 1)
 
     halves = [pl.ds(i * HALF, HALF) for i in range(2)]
 
@@ -122,12 +131,20 @@
             copies.append(send(block, kv[w].at[3, half], left))
         return copies
 
-    def relay(w, i, near):
-        near[2 * i].wait_recv()
-        from_left = send(kv[w].at[1, halves[i]], kv[w].at[0, halves[i]], right)
-        near[2 * i + 1].wait_recv()
-        from_right = send(kv[w].at[3, halves[i]], kv[w].at[4, halves[i]], left)
-        return [from_left, from_right]
+    def plan_relay(w):
+        copies = []
+        for half in halves:
+            copies.append(prepare(kv[w].at[1, half], kv[w].at[0, half], right))
+            copies.append(prepare(kv[w].at[3, half], kv[w].at[4, half], left))
+        return copies
+
+    def relay(h, near, far, when):
+        for side in range(2):
+
+            @pl.when(when[side])
+            def _():
+                near[2 * h + side].wait_recv()
+                far[2 * h + side].start()
 
     def share_near(w):
         return [send(kv[w].at[1], kv[w].at[7], sibling), send(kv[w].at[3], kv[w].at[6], sibling)]
@@ -157,11 +174,15 @@
         next_round()
         a2a_p += exchange(proj, pk, PACK, peers[2 * distance : 2 * distance + 2])
     a2a_g += exchange(gout, dk, OUT, peers)
-    far_k = relay(0, 0, near_k)
-    far_k += relay(0, 1, near_k)
+    far_k, far_v = plan_relay(0), plan_relay(1)
+    for near, far in ((near_k, far_k), (near_v, far_v)):
+        for h in range(2):
+            relay(h, near, far, fast)
+    for h in range(2):
+        relay(h, near_k, far_k, slow)
     sib_k += share_near(0)
-    far_v = relay(1, 0, near_v)
-    far_v += relay(1, 1, near_v)
+    for h in range(2):
+        relay(h, near_v, far_v, slow)
     sib_v += share_near(1)
 
     def spread(picked, window):
@@ -256,17 +277,22 @@
             copies.append(send(far_send.at[w, 1, half], far_recv.at[w, 1, half], left))
         return copies
 
-    def to_near(w, h, sib, far):
+    def plan_near(w):
+        copies = []
+        for half in halves:
+            copies += [prepare(near_send.at[w, i, half], near_recv.at[w, i, half], (right, left)[i]) for i in range(2)]
+        return copies
+
+    def to_near(w, h, sib, far, near, when):
         half = halves[h]
-        copies = []
-        for i, device in enumerate((right, left)):
-            if h == 0:
-                sib[2 - 2 * i].wait_recv()
-            part = summed(w, 2 - 4 * i, half) + sib_recv[w, 2 - 2 * i, half].astype(F32)
-            far[2 * h + i].wait_recv()
-            near_send[w, i, half] = (part + far_recv[w, i, half].astype(F32)).astype(BF16)
-            copies.append(send(near_send.at[w, i, half], near_recv.at[w, i, half], device))
-        return copies
+        for i in range(2):
+
+            @pl.when(when[i])
+            def _():
+                part = summed(w, 2 - 4 * i, half) + sib_recv[w, 2 - 2 * i, half].astype(F32)
+                far[2 * h + i].wait_recv()
+                near_send[w, i, half] = (part + far_recv[w, i, half].astype(F32)).astype(BF16)
+                near[2 * h + i].start()
 
     def finish(w, h, sib, near):
         half = halves[h]
@@ -287,8 +313,8 @@
         own.start()
         return copies, own
 
+    sib_k += share_far(0, far_k)
     gather_proj()
-    sib_k += share_far(0, far_k)
     own_kv[0].wait()
     for copy in sib_k:
         copy.wait_recv()
@@ -309,14 +335,22 @@
     for s in range(SEGS):
         key_terms(s)
     key_sib = to_sibling(0)
+    value_near, key_near = plan_near(1), plan_near(0)
+    value_sib[0].wait_recv()
+    value_sib[2].wait_recv()
+    to_near(1, 0, value_sib, value_far, value_near, fast)
     for s in range(SEGS):
         query_terms(s)
     grad_copies, grad_own = give_back(win_g, dproj_send, dproj_out, PACK, 1)
     key_far = to_far(0, key_sib)
-    value_near = to_near(1, 0, value_sib, value_far)
-    value_near += to_near(1, 1, value_sib, value_far)
-    key_near = to_near(0, 0, key_sib, key_far)
-    key_near += to_near(0, 1, key_sib, key_far)
+    to_near(1, 1, value_sib, value_far, value_near, fast)
+    for h in range(2):
+        to_near(1, h, value_sib, value_far, value_near, slow)
+    key_sib[0].wait_recv()
+    key_sib[2].wait_recv()
+    for when in (fast, slow):
+        for h in range(2):
+            to_near(0, h, key_sib, key_far, key_near, when)
     finish(1, 0, value_sib, value_near)
     finish(1, 1, value_sib, value_near)
     finish(0, 0, key_sib, key_near)

time: 50.7 us -> 49 us (0.966)
  Pallas kernels: 49.9 us -> 48.2 us
    pallas_call x1, Pallas kernels: 49 us -> 47.4 us  [local(): pl.pallas_call(kernel, out_shape=tuple((pltpu.VMEM(r.shape, BF16) for r i...]
where the time goes in v5:
time: 49 us; the launch traced here: 48.9 us
  Pallas kernels  48.2 us (98%)
  between operations  0.64 us (1%)
    pallas_call x1, Pallas kernels, local(): pl.pallas_call(kernel, out_shape=tuple((pltpu.VMEM(r.shape, BF16) for r i...  47.4 us

profile of v5, /device:TPU:1, one launch (start us, length us, event | category | flops | bytes accessed | tf_op | source)
XLA Modules:
  0.0 48.9 jit_solution(3071821388607911933)
XLA Ops:
  0.6 47.4 %shard_map.76 = (bf16[16,5120]{1,0:T(8,128)(2,1)S(1)}, bf16[16,7168]{1,0:T(8,128)(2,1)S(1)}, bf16[512,256]{1,0:T(8,128)(2,1)S(1)}) custom-call(s32[1,128]{1,0:T(1,128)} %ids_hbm.1, s32[1,4]{1,0:T(1,128)} %owner_hbm.1, bf16[16,7168]{1,0:T(8,128)(2,1)} %proj.1, bf16[16,5120]{1,0:T(8,128)(2,1)} %gout.1, bf16[512,256]{1,0:T(8,128)(2,1)} %cache.1), custom_call_target="tpu_custom_call" | custom-call | tf_op jit(solution)/shard_map/pallas_call | solution.py:387
  48.0 0.9 %shard_map.77 = (bf16[16,5120]{1,0:T(8,128)(2,1)}, bf16[16,7168]{1,0:T(8,128)(2,1)}, bf16[512,256]{1,0:T(8,128)(2,1)}) custom-call(bf16[16,5120]{1,0:T(8,128)(2,1)S(1)} %get-tuple-element.6.att, bf16[16,7168]{1,0:T(8,128)(2,1)S(1)} %get-tuple-element.7.dproj, bf16[512,256]{1,0:T(8,128)(2,1)S(1)} %get-tuple-element.8.dcache), custom_call_target="tpu_custom_call" | custom-call | tf_op jit(solution)/shard_map/pallas_call | solution.py:425

commit v6 on v5

--- a/solution.py
+++ b/solution.py
@@ -169,11 +169,13 @@
         return [send(block.at[:, columns(p, width)], staged.at[head], (dp, p)) for p in chosen]
 
     a2a_p = exchange(proj, pk, PACK, peers[:2])
-    a2a_g = []
+    a2a_g = exchange(gout, dk, OUT, peers[:2])
     for distance in range(1, 4):
         next_round()
         a2a_p += exchange(proj, pk, PACK, peers[2 * distance : 2 * distance + 2])
-    a2a_g += exchange(gout, dk, OUT, peers)
+        if distance == 1:
+            a2a_g += exchange(gout, dk, OUT, peers[2:4])
+    a2a_g += exchange(gout, dk, OUT, peers[4:])
     far_k, far_v = plan_relay(0), plan_relay(1)
     for near, far in ((near_k, far_k), (near_v, far_v)):
         for h in range(2):
@@ -267,13 +269,14 @@
         return copies
 
     def to_far(w, sib):
+        own = [[summed(w, 4, half), summed(w, -4, half)] for half in halves]
         sib[3].wait_recv()
         copies = []
-        for half in halves:
+        for (own_right, own_left), half in zip(own, halves):
             extra = sib_recv[w, 3, half].astype(F32)
-            far_send[w, 0, half] = (summed(w, 4, half) + jnp.where(core == 0, extra, 0.0)).astype(BF16)
+            far_send[w, 0, half] = (own_right + jnp.where(core == 0, extra, 0.0)).astype(BF16)
             copies.append(send(far_send.at[w, 0, half], far_recv.at[w, 0, half], right))
-            far_send[w, 1, half] = (summed(w, -4, half) + jnp.where(core == 1, extra, 0.0)).astype(BF16)
+            far_send[w, 1, half] = (own_left + jnp.where(core == 1, extra, 0.0)).astype(BF16)
             copies.append(send(far_send.at[w, 1, half], far_recv.at[w, 1, half], left))
         return copies
 
@@ -331,10 +334,10 @@
         copy.wait_recv()
     for s in range(SEGS):
         attend(s)
-    att_copies, att_own = give_back(win_o, att_send, att_out, OUT, 0)
     for s in range(SEGS):
         key_terms(s)
     key_sib = to_sibling(0)
+    att_copies, att_own = give_back(win_o, att_send, att_out, OUT, 0)
     value_near, key_near = plan_near(1), plan_near(0)
     value_sib[0].wait_recv()
     value_sib[2].wait_recv()

time: 49 us -> 48.7 us (level)
  no operation moved by 1% of the time
where the time goes in v6:
time: 48.7 us; the launch traced here: 48.6 us
  Pallas kernels  47.9 us (98%)
  between operations  0.64 us (1%)
    pallas_call x1, Pallas kernels, local(): pl.pallas_call(kernel, out_shape=tuple((pltpu.VMEM(r.shape, BF16) for r i...  47.1 us

profile of v6, /device:TPU:1, one launch (start us, length us, event | category | flops | bytes accessed | tf_op | source)
XLA Modules:
  0.0 48.6 jit_solution(16213616056074011016)
XLA Ops:
  0.6 47.1 %shard_map.76 = (bf16[16,5120]{1,0:T(8,128)(2,1)S(1)}, bf16[16,7168]{1,0:T(8,128)(2,1)S(1)}, bf16[512,256]{1,0:T(8,128)(2,1)S(1)}) custom-call(s32[1,128]{1,0:T(1,128)} %ids_hbm.1, s32[1,4]{1,0:T(1,128)} %owner_hbm.1, bf16[16,7168]{1,0:T(8,128)(2,1)} %proj.1, bf16[16,5120]{1,0:T(8,128)(2,1)} %gout.1, bf16[512,256]{1,0:T(8,128)(2,1)} %cache.1), custom_call_target="tpu_custom_call" | custom-call | tf_op jit(solution)/shard_map/pallas_call | solution.py:390
  47.7 0.9 %shard_map.77 = (bf16[16,5120]{1,0:T(8,128)(2,1)}, bf16[16,7168]{1,0:T(8,128)(2,1)}, bf16[512,256]{1,0:T(8,128)(2,1)}) custom-call(bf16[16,5120]{1,0:T(8,128)(2,1)S(1)} %get-tuple-element.6.att, bf16[16,7168]{1,0:T(8,128)(2,1)S(1)} %get-tuple-element.7.dproj, bf16[512,256]{1,0:T(8,128)(2,1)S(1)} %get-tuple-element.8.dcache), custom_call_target="tpu_custom_call" | custom-call | tf_op jit(solution)/shard_map/pallas_call | solution.py:428

commit v7 on v6

--- a/solution.py
+++ b/solution.py
@@ -173,9 +173,7 @@
     for distance in range(1, 4):
         next_round()
         a2a_p += exchange(proj, pk, PACK, peers[2 * distance : 2 * distance + 2])
-        if distance == 1:
-            a2a_g += exchange(gout, dk, OUT, peers[2:4])
-    a2a_g += exchange(gout, dk, OUT, peers[4:])
+        a2a_g += exchange(gout, dk, OUT, peers[2 * distance : 2 * distance + 2])
     far_k, far_v = plan_relay(0), plan_relay(1)
     for near, far in ((near_k, far_k), (near_v, far_v)):
         for h in range(2):

time: 48.7 us -> 48.7 us (level)
  no operation moved by 1% of the time
where the time goes in v7:
time: 48.7 us; the launch traced here: 48.6 us
  Pallas kernels  47.9 us (98%)
  between operations  0.64 us (1%)
    pallas_call x1, Pallas kernels, local(): pl.pallas_call(kernel, out_shape=tuple((pltpu.VMEM(r.shape, BF16) for r i...  47.1 us

profile of v7, /device:TPU:1, one launch (start us, length us, event | category | flops | bytes accessed | tf_op | source)
XLA Modules:
  0.0 48.6 jit_solution(10560326086826786547)
XLA Ops:
  0.6 47.1 %shard_map.76 = (bf16[16,5120]{1,0:T(8,128)(2,1)S(1)}, bf16[16,7168]{1,0:T(8,128)(2,1)S(1)}, bf16[512,256]{1,0:T(8,128)(2,1)S(1)}) custom-call(s32[1,128]{1,0:T(1,128)} %ids_hbm.1, s32[1,4]{1,0:T(1,128)} %owner_hbm.1, bf16[16,7168]{1,0:T(8,128)(2,1)} %proj.1, bf16[16,5120]{1,0:T(8,128)(2,1)} %gout.1, bf16[512,256]{1,0:T(8,128)(2,1)} %cache.1), custom_call_target="tpu_custom_call" | custom-call | tf_op jit(solution)/shard_map/pallas_call | solution.py:388
  47.7 0.9 %shard_map.77 = (bf16[16,5120]{1,0:T(8,128)(2,1)}, bf16[16,7168]{1,0:T(8,128)(2,1)}, bf16[512,256]{1,0:T(8,128)(2,1)}) custom-call(bf16[16,5120]{1,0:T(8,128)(2,1)S(1)} %get-tuple-element.6.att, bf16[16,7168]{1,0:T(8,128)(2,1)S(1)} %get-tuple-element.7.dproj, bf16[512,256]{1,0:T(8,128)(2,1)S(1)} %get-tuple-element.8.dcache), custom_call_target="tpu_custom_call" | custom-call | tf_op jit(solution)/shard_map/pallas_call | solution.py:426
